TPU v7x, 32 devices: a whole 2x2x4 slice. The times are simulated.
32 devices in a mesh: dp: 8 (over z, x), fsdp: 4 (over y, core).
Axes of the slice: x: 2, y: 2, z: 4, core: 2. Of those that a mesh axis runs over, the one named last changes fastest.
Arguments:
- tokens: bfloat16 [16384, 1024], P(('dp', 'fsdp')), may hold values from -6 to 6
- segment: int32 [32, 512], P(('dp', 'fsdp')), may hold values from -1 to 5, as said below
- cotangent: bfloat16 [16384, 1024], P(('dp', 'fsdp')), may hold values from -6 to 6
- query_w: float32 [1024, 1024], P(('dp', 'fsdp')), may hold values from -0.1875 to 0.1875
- key_w: float32 [1024, 1024], P(('dp', 'fsdp')), may hold values from -0.1875 to 0.1875
- value_w: float32 [1024, 1024], P(('dp', 'fsdp')), may hold values from -0.1875 to 0.1875
- attn_out_w: float32 [1024, 1024], P(('dp', 'fsdp')), may hold values from -0.75 to 0.75
- up_w: float32 [1024, 4096], P(('dp', 'fsdp')), may hold values from -0.1875 to 0.1875
- down_w: float32 [4096, 1024], P(None, ('dp', 'fsdp')), may hold values from -0.09375 to 0.09375
- query_bias: float32 [1024], P(('dp', 'fsdp')), may hold values from -3 to 3
- value_bias: float32 [1024], P(('dp', 'fsdp')), may hold values from -2 to 2
- attn_out_bias: float32 [1024], P(('dp', 'fsdp')), may hold values from -2 to 2
- up_bias: float32 [4096], P(('dp', 'fsdp')), may hold values from -2 to 2
- down_bias: float32 [1024], P(('dp', 'fsdp')), may hold values from -2 to 2
- norm1_gain: float32 [1024], P(('dp', 'fsdp')), may hold values from 0.5 to 1.5
- norm1_shift: float32 [1024], P(('dp', 'fsdp')), may hold values from -2 to 2
- norm2_gain: float32 [1024], P(('dp', 'fsdp')), may hold values from 0.5 to 1.5
- norm2_shift: float32 [1024], P(('dp', 'fsdp')), may hold values from -2 to 2
Outputs:
- outputs: bfloat16 [16384, 1024], P(('dp', 'fsdp'))
- d_tokens: float32 [16384, 1024], P(('dp', 'fsdp'))
- d_query_w: float32 [1024, 1024], P(('dp', 'fsdp'))
- d_key_w: float32 [1024, 1024], P(('dp', 'fsdp'))
- d_value_w: float32 [1024, 1024], P(('dp', 'fsdp'))
- d_attn_out_w: float32 [1024, 1024], P(('dp', 'fsdp'))
- d_up_w: float32 [1024, 4096], P(('dp', 'fsdp'))
- d_down_w: float32 [4096, 1024], P(None, ('dp', 'fsdp'))
- d_query_bias: float32 [1024], P(('dp', 'fsdp'))
- d_value_bias: float32 [1024], P(('dp', 'fsdp'))
- d_attn_out_bias: float32 [1024], P(('dp', 'fsdp'))
- d_up_bias: float32 [4096], P(('dp', 'fsdp'))
- d_down_bias: float32 [1024], P(('dp', 'fsdp'))
- d_norm1_gain: float32 [1024], P(('dp', 'fsdp'))
- d_norm1_shift: float32 [1024], P(('dp', 'fsdp'))
- d_norm2_gain: float32 [1024], P(('dp', 'fsdp'))
- d_norm2_shift: float32 [1024], P(('dp', 'fsdp'))
Inputs may be any that keep to these rules, and one draw needn't show every extreme that they name: `segment`: within each row, ids start at 0 and never fall over its real tokens; padding tokens hold -1 and stand only at a row's end; every row has real tokens.
All inputs are finite; a program needn't handle non-finite values.
Results may differ from a plain program's by a relative error of at most 0.02.
Values may be sent and summed in bfloat16 or wider, within the bound.
A program may use at most 192 MiB of HBM per device.

v0:
```python
import jax
import jax.numpy as jnp
from jax import lax
from jax.sharding import PartitionSpec as P

HEAD = 64


norm_epsilon = 1e-12
masked_score = -1000000000.0


def to_half(array):
    return array.astype(jnp.bfloat16)


def matmul(left, right):
    return jnp.dot(left, right, preferred_element_type=jnp.float32)


def matmul_nt(left, right):
    return lax.dot_general(
        left, right, (((1,), (1,)), ((), ())), preferred_element_type=jnp.float32
    )


def contract_rows(left, right):
    return lax.dot_general(
        left, right, (((0,), (0,)), ((), ())), preferred_element_type=jnp.float32
    )


def column_sums(array):
    return jnp.sum(array.astype(jnp.float32), axis=0)


def normalize(values, gain_vec, shift_vec):
    center = values - jnp.mean(values, axis=-1, keepdims=True)
    spread = jnp.mean(center * center, axis=-1, keepdims=True)
    return center * lax.rsqrt(spread + norm_epsilon) * gain_vec + shift_vec


def gelu_exact(values):
    return jax.nn.gelu(values, approximate=False)


def split_heads(block):
    return block.reshape(block.shape[0], -1, HEAD)


def row_scores(queries, key_rows, labels):
    scores = (
        jnp.einsum("qhe,khe->hqk", queries, key_rows, preferred_element_type=jnp.float32) * 0.125
    )
    allowed = labels[:, None] == labels[None, :]
    return jnp.where(allowed[None], scores, masked_score)


def attend_row(pieces):
    queries, key_rows, value_rows, labels = pieces
    scores = row_scores(split_heads(queries), split_heads(key_rows), labels)
    row_max = jnp.max(scores, axis=-1, keepdims=True)
    row_exp = jnp.exp(scores - row_max)
    row_total = jnp.sum(row_exp, axis=-1, keepdims=True)
    probs_half = to_half(row_exp / row_total)
    context = jnp.einsum(
        "hqk,khe->qhe", probs_half, split_heads(value_rows), preferred_element_type=jnp.float32
    )
    return (to_half(context.reshape(queries.shape)), (row_max + jnp.log(row_total))[..., 0])


def attend_back(pieces):
    queries, key_rows, value_rows, labels, log_total, d_context = pieces
    query_heads = split_heads(queries)
    key_heads = split_heads(key_rows)
    context_heads = split_heads(d_context)
    scores = row_scores(query_heads, key_heads, labels)
    attn_probs = jnp.exp(scores - log_total[..., None])
    d_probs = jnp.einsum(
        "qhe,khe->hqk", context_heads, split_heads(value_rows), preferred_element_type=jnp.float32
    )
    row_delta = jnp.sum(attn_probs * d_probs, axis=-1, keepdims=True)
    d_scores = to_half(attn_probs * (d_probs - row_delta))
    d_queries = (
        jnp.einsum("hqk,khe->qhe", d_scores, key_heads, preferred_element_type=jnp.float32) * 0.125
    )
    d_keys = (
        jnp.einsum("hqk,qhe->khe", d_scores, query_heads, preferred_element_type=jnp.float32)
        * 0.125
    )
    d_values = jnp.einsum(
        "hqk,qhe->khe", to_half(attn_probs), context_heads, preferred_element_type=jnp.float32
    )
    return (
        to_half(d_queries.reshape(queries.shape)),
        to_half(d_keys.reshape(queries.shape)),
        to_half(d_values.reshape(queries.shape)),
    )


def per_device(
    tokens,
    segment,
    cotangent,
    query_w,
    key_w,
    value_w,
    attn_out_w,
    up_w,
    down_w,
    query_bias,
    value_bias,
    attn_out_bias,
    up_bias,
    down_bias,
    norm1_gain,
    norm1_shift,
    norm2_gain,
    norm2_shift,
):
    row_count = segment.shape[0]
    row_length = segment.shape[1]
    model_width = tokens.shape[1]

    def by_rows(array):
        return array.reshape(row_count, row_length, -1)

    attn_set = (
        lax.all_gather(to_half(query_w), ("dp", "fsdp"), axis=0, tiled=True),
        lax.all_gather(to_half(key_w), ("dp", "fsdp"), axis=0, tiled=True),
        lax.all_gather(to_half(value_w), ("dp", "fsdp"), axis=0, tiled=True),
        lax.all_gather(to_half(attn_out_w), ("dp", "fsdp"), axis=0, tiled=True),
        lax.all_gather(to_half(query_bias), ("dp", "fsdp"), axis=0, tiled=True),
        lax.all_gather(to_half(value_bias), ("dp", "fsdp"), axis=0, tiled=True),
        lax.all_gather(to_half(attn_out_bias), ("dp", "fsdp"), axis=0, tiled=True),
        lax.all_gather(to_half(norm1_gain), ("dp", "fsdp"), axis=0, tiled=True),
        lax.all_gather(to_half(norm1_shift), ("dp", "fsdp"), axis=0, tiled=True),
    )
    wq_full, wk_full, wv_full, wo_full, bias_q, bias_v, bias_o, gain_one, shift_one = attn_set
    ffn_set = (
        lax.all_gather(to_half(up_w), ("dp", "fsdp"), axis=0, tiled=True),
        lax.all_gather(to_half(down_w), ("dp", "fsdp"), axis=1, tiled=True),
        lax.all_gather(to_half(up_bias), ("dp", "fsdp"), axis=0, tiled=True),
        lax.all_gather(to_half(down_bias), ("dp", "fsdp"), axis=0, tiled=True),
        lax.all_gather(to_half(norm2_gain), ("dp", "fsdp"), axis=0, tiled=True),
        lax.all_gather(to_half(norm2_shift), ("dp", "fsdp"), axis=0, tiled=True),
    )
    w_up, w_down, bias_up, bias_down, gain_two, shift_two = ffn_set
    queries = to_half(matmul(tokens, wq_full) + bias_q.astype(jnp.float32))
    key_rows = to_half(matmul(tokens, wk_full))
    value_rows = to_half(matmul(tokens, wv_full) + bias_v.astype(jnp.float32))
    context, log_total = lax.map(
        attend_row, (by_rows(queries), by_rows(key_rows), by_rows(value_rows), segment)
    )
    context = context.reshape(-1, model_width)
    attended = matmul(context, wo_full) + bias_o.astype(jnp.float32)
    first_sum = tokens.astype(jnp.float32) + attended
    norm_mid, pull_one = jax.vjp(
        normalize, first_sum, gain_one.astype(jnp.float32), shift_one.astype(jnp.float32)
    )
    mid_half = to_half(norm_mid)
    pre_act = matmul(mid_half, w_up) + bias_up.astype(jnp.float32)
    act_out, pull_act = jax.vjp(gelu_exact, pre_act)
    act_half = to_half(act_out)
    ffn_out = matmul(act_half, w_down) + bias_down.astype(jnp.float32)
    second_sum = mid_half.astype(jnp.float32) + ffn_out
    final, pull_two = jax.vjp(
        normalize, second_sum, gain_two.astype(jnp.float32), shift_two.astype(jnp.float32)
    )
    outputs = to_half(final)
    valid = (segment.reshape(-1) >= 0).astype(jnp.float32)[:, None]
    d_out = cotangent.astype(jnp.float32) * valid
    d_second, d_gain_two, d_shift_two = pull_two(d_out)
    up_back, down_back = (
        lax.all_gather(to_half(up_w), ("dp", "fsdp"), axis=0, tiled=True),
        lax.all_gather(to_half(down_w), ("dp", "fsdp"), axis=1, tiled=True),
    )
    d_ffn = to_half(d_second)
    d_down_turned = contract_rows(d_ffn, act_half)
    d_down_bias = column_sums(d_ffn)
    (d_pre,) = pull_act(matmul_nt(d_ffn, down_back))
    d_pre_half = to_half(d_pre)
    d_up_w = contract_rows(mid_half, d_pre_half)
    d_up_bias = column_sums(d_pre_half)
    d_mid = d_second + matmul_nt(d_pre_half, up_back)
    d_first, d_gain_one, d_shift_one = pull_one(d_mid)
    wq_back, wk_back, wv_back, wo_back = (
        lax.all_gather(to_half(query_w), ("dp", "fsdp"), axis=0, tiled=True),
        lax.all_gather(to_half(key_w), ("dp", "fsdp"), axis=0, tiled=True),
        lax.all_gather(to_half(value_w), ("dp", "fsdp"), axis=0, tiled=True),
        lax.all_gather(to_half(attn_out_w), ("dp", "fsdp"), axis=0, tiled=True),
    )
    d_att = to_half(d_first)
    d_attn_out_w = contract_rows(context, d_att)
    d_attn_out_bias = column_sums(d_att)
    d_context = to_half(matmul_nt(d_att, wo_back))
    d_queries, d_keys, d_values = lax.map(
        attend_back,
        (
            by_rows(queries),
            by_rows(key_rows),
            by_rows(value_rows),
            segment,
            log_total,
            by_rows(d_context),
        ),
    )
    d_queries = d_queries.reshape(-1, model_width)
    d_keys = d_keys.reshape(-1, model_width)
    d_values = d_values.reshape(-1, model_width)
    d_query_w = contract_rows(tokens, d_queries)
    d_key_w = contract_rows(tokens, d_keys)
    d_value_w = contract_rows(tokens, d_values)
    d_query_bias = column_sums(d_queries)
    d_value_bias = column_sums(d_values)
    d_tokens = (
        d_first
        + matmul_nt(d_queries, wq_back)
        + matmul_nt(d_keys, wk_back)
        + matmul_nt(d_values, wv_back)
    )
    members = (
        d_query_w,
        d_key_w,
        d_value_w,
        d_attn_out_w,
        d_up_w,
        d_down_turned,
        d_query_bias,
        d_value_bias,
        d_attn_out_bias,
        d_up_bias,
        d_down_bias,
        d_gain_one,
        d_shift_one,
        d_gain_two,
        d_shift_two,
    )
    block_sums = (
        lax.psum_scatter(
            members[0].astype(jnp.bfloat16), "dp", scatter_dimension=0, tiled=True
        ).astype(jnp.float32),
        lax.psum_scatter(
            members[1].astype(jnp.bfloat16), "dp", scatter_dimension=0, tiled=True
        ).astype(jnp.float32),
        lax.psum_scatter(
            members[2].astype(jnp.bfloat16), "dp", scatter_dimension=0, tiled=True
        ).astype(jnp.float32),
        lax.psum_scatter(
            members[3].astype(jnp.bfloat16), "dp", scatter_dimension=0, tiled=True
        ).astype(jnp.float32),
        lax.psum_scatter(
            members[4].astype(jnp.bfloat16), "dp", scatter_dimension=0, tiled=True
        ).astype(jnp.float32),
        lax.psum_scatter(
            members[5].astype(jnp.bfloat16), "dp", scatter_dimension=0, tiled=True
        ).astype(jnp.float32),
        lax.psum_scatter(
            members[6].astype(jnp.bfloat16), "dp", scatter_dimension=0, tiled=True
        ).astype(jnp.float32),
        lax.psum_scatter(
            members[7].astype(jnp.bfloat16), "dp", scatter_dimension=0, tiled=True
        ).astype(jnp.float32),
        lax.psum_scatter(
            members[8].astype(jnp.bfloat16), "dp", scatter_dimension=0, tiled=True
        ).astype(jnp.float32),
        lax.psum_scatter(
            members[9].astype(jnp.bfloat16), "dp", scatter_dimension=0, tiled=True
        ).astype(jnp.float32),
        lax.psum_scatter(
            members[10].astype(jnp.bfloat16), "dp", scatter_dimension=0, tiled=True
        ).astype(jnp.float32),
        lax.psum_scatter(
            members[11].astype(jnp.bfloat16), "dp", scatter_dimension=0, tiled=True
        ).astype(jnp.float32),
        lax.psum_scatter(
            members[12].astype(jnp.bfloat16), "dp", scatter_dimension=0, tiled=True
        ).astype(jnp.float32),
        lax.psum_scatter(
            members[13].astype(jnp.bfloat16), "dp", scatter_dimension=0, tiled=True
        ).astype(jnp.float32),
        lax.psum_scatter(
            members[14].astype(jnp.bfloat16), "dp", scatter_dimension=0, tiled=True
        ).astype(jnp.float32),
    )
    every_shard = (
        lax.psum_scatter(
            block_sums[0].astype(jnp.bfloat16), "fsdp", scatter_dimension=0, tiled=True
        ).astype(jnp.float32),
        lax.psum_scatter(
            block_sums[1].astype(jnp.bfloat16), "fsdp", scatter_dimension=0, tiled=True
        ).astype(jnp.float32),
        lax.psum_scatter(
            block_sums[2].astype(jnp.bfloat16), "fsdp", scatter_dimension=0, tiled=True
        ).astype(jnp.float32),
        lax.psum_scatter(
            block_sums[3].astype(jnp.bfloat16), "fsdp", scatter_dimension=0, tiled=True
        ).astype(jnp.float32),
        lax.psum_scatter(
            block_sums[4].astype(jnp.bfloat16), "fsdp", scatter_dimension=0, tiled=True
        ).astype(jnp.float32),
        lax.psum_scatter(
            block_sums[5].astype(jnp.bfloat16), "fsdp", scatter_dimension=0, tiled=True
        ).astype(jnp.float32),
        lax.psum_scatter(
            block_sums[6].astype(jnp.bfloat16), "fsdp", scatter_dimension=0, tiled=True
        ).astype(jnp.float32),
        lax.psum_scatter(
            block_sums[7].astype(jnp.bfloat16), "fsdp", scatter_dimension=0, tiled=True
        ).astype(jnp.float32),
        lax.psum_scatter(
            block_sums[8].astype(jnp.bfloat16), "fsdp", scatter_dimension=0, tiled=True
        ).astype(jnp.float32),
        lax.psum_scatter(
            block_sums[9].astype(jnp.bfloat16), "fsdp", scatter_dimension=0, tiled=True
        ).astype(jnp.float32),
        lax.psum_scatter(
            block_sums[10].astype(jnp.bfloat16), "fsdp", scatter_dimension=0, tiled=True
        ).astype(jnp.float32),
        lax.psum_scatter(
            block_sums[11].astype(jnp.bfloat16), "fsdp", scatter_dimension=0, tiled=True
        ).astype(jnp.float32),
        lax.psum_scatter(
            block_sums[12].astype(jnp.bfloat16), "fsdp", scatter_dimension=0, tiled=True
        ).astype(jnp.float32),
        lax.psum_scatter(
            block_sums[13].astype(jnp.bfloat16), "fsdp", scatter_dimension=0, tiled=True
        ).astype(jnp.float32),
        lax.psum_scatter(
            block_sums[14].astype(jnp.bfloat16), "fsdp", scatter_dimension=0, tiled=True
        ).astype(jnp.float32),
    )
    (
        shard_qw,
        shard_kw,
        shard_vw,
        shard_ow,
        shard_uw,
        shard_turned,
        shard_qb,
        shard_vb,
        shard_ob,
        shard_ub,
        shard_db,
        shard_g1,
        shard_s1,
        shard_g2,
        shard_s2,
    ) = every_shard
    shard_dw = jnp.transpose(shard_turned)
    return (
        outputs,
        d_tokens,
        shard_qw,
        shard_kw,
        shard_vw,
        shard_ow,
        shard_uw,
        shard_dw,
        shard_qb,
        shard_vb,
        shard_ob,
        shard_ub,
        shard_db,
        shard_g1,
        shard_s1,
        shard_g2,
        shard_s2,
    )


def solution(mesh):
    in_specs = (
        P(("dp", "fsdp"), None),
        P(("dp", "fsdp"), None),
        P(("dp", "fsdp"), None),
        P(("dp", "fsdp"), None),
        P(("dp", "fsdp"), None),
        P(("dp", "fsdp"), None),
        P(("dp", "fsdp"), None),
        P(("dp", "fsdp"), None),
        P(None, ("dp", "fsdp")),
        P(("dp", "fsdp")),
        P(("dp", "fsdp")),
        P(("dp", "fsdp")),
        P(("dp", "fsdp")),
        P(("dp", "fsdp")),
        P(("dp", "fsdp")),
        P(("dp", "fsdp")),
        P(("dp", "fsdp")),
        P(("dp", "fsdp")),
    )
    out_specs = (
        P(("dp", "fsdp"), None),
        P(("dp", "fsdp"), None),
        P(("dp", "fsdp"), None),
        P(("dp", "fsdp"), None),
        P(("dp", "fsdp"), None),
        P(("dp", "fsdp"), None),
        P(("dp", "fsdp"), None),
        P(None, ("dp", "fsdp")),
        P(("dp", "fsdp")),
        P(("dp", "fsdp")),
        P(("dp", "fsdp")),
        P(("dp", "fsdp")),
        P(("dp", "fsdp")),
        P(("dp", "fsdp")),
        P(("dp", "fsdp")),
        P(("dp", "fsdp")),
        P(("dp", "fsdp")),
    )
    return jax.shard_map(
        per_device, mesh=mesh, in_specs=in_specs, out_specs=out_specs, check_vma=False
    )
```

profile of v0, /device:TPU:0, one launch (start us, length us, event | category | flops | bytes accessed | tf_op | source)
XLA Modules:
  0.0 1218.3 jit_solution(10022716797260508426)
XLA Ops:
  24.3 42.4 %all-reduce.26 = (bf16[1024]{0:T(1024)(128)(2,1)S(1)}, bf16[1024]{0:T(1024)(128)(2,1)S(1)}, bf16[1024]{0:T(1024)(128)(2,1)S(1)}, bf16[1024]{0:T(1024)(128)(2,1)S...) all-reduce(bf16[1024]{0:T(1024)(128)(2,1)S(1)} %dynamic-update-slic, ...), channel_id=1, replica_groups=mesh['dp'=8,'fsdp'=4] {'dp','fsdp'}, use_global_device_ids=true, to_apply=%add | all-reduce | flops 8192 | bytes 32768
  67.4 40.3 %all-gather = bf16[32,1,128]{2,1,0:T(2,128)(2,1)S(1)} all-gather(bf16[1,1,128]{2,1,0:T(2,128)(2,1)S(1)} %convert_bitcast_fusion.4), channel_id=1, replica_groups=mesh['dp'=8,'fsdp'=4] {'dp','fsdp'}, dimensions={0}, use_global_device_ids=true | all-gather | bytes 8448 | tf_op jit(solution)/shard_map/all_gather | solution.py:143
  113.3 16.1 %all-gather.10.cloned.1.call-done = bf16[1024,1024]{1,0:T(8,128)(2,1)} async-done(((bf16[32,1024]{1,0:T(8,128)(2,1)}), bf16[1024,1024]{1,0:T(8,128)(2,1)}) %all-gather.10.cloned.1.call-update) | async-done | bytes 2097168 | tf_op jit(solution)/shard_map/all_gather | solution.py:129
  132.8 55.3 %all-gather.12.cloned.1.call-done = bf16[1024,1024]{1,0:T(8,128)(2,1)} async-done(((bf16[32,1024]{1,0:T(8,128)(2,1)}), bf16[1024,1024]{1,0:T(8,128)(2,1)}) %all-gather.12.cloned.1.call-update) | async-done | bytes 2097168 | tf_op jit(solution)/shard_map/all_gather | solution.py:130
  218.1 28.6 %all-gather.14.cloned.1.call-done = bf16[1024,1024]{1,0:T(8,128)(2,1)} async-done(((bf16[32,1024]{1,0:T(8,128)(2,1)}), bf16[1024,1024]{1,0:T(8,128)(2,1)}) %all-gather.14.cloned.1.call-update) | async-done | bytes 2097168 | tf_op jit(solution)/shard_map/all_gather | solution.py:132
  251.6 74.9 %all-gather.16.cloned.1.call-done = bf16[1024,4096]{1,0:T(8,128)(2,1)} async-done(((bf16[32,4096]{1,0:T(8,128)(2,1)}), bf16[1024,4096]{1,0:T(8,128)(2,1)}) %all-gather.16.cloned.1.call-update) | async-done | bytes 8388624 | tf_op jit(solution)/shard_map/all_gather | solution.py:141
  326.5 27.9 %multiply_convert_fusion.1 = (bf16[512,4096]{1,0:T(8,128)(2,1)}, f32[512,4096]{1,0:T(8,128)}, f32[512,4096]{1,0:T(8,128)}) fusion(f32[4096]{0:T(1024)S(1)} %bitcast.100, bf16[1024,4096]{1,0:T(8,128)(2,1)} %all-gather.16.cloned.1.call-done, f32[512,1024]{1,0:T(8,128)S(1)} %get-tuple-element.167, f32[1024]{0:T(1024)S(1)} %convert_element_type.323, ...), kind=kOutput, calls=%fused_computation.13 | convolution fusion | flops 4436000768 | bytes 31485952 | tf_op jit(solution)/shard_map/dot_general | solution.py:18
  354.3 51.6 %all-gather.18.cloned.1.call-done = bf16[4096,1024]{0,1:T(8,128)(2,1)} async-done(((bf16[4096,32]{0,1:T(8,128)(2,1)}), bf16[4096,1024]{0,1:T(8,128)(2,1)}) %all-gather.18.cloned.1.call-update) | async-done | bytes 8388624 | tf_op jit(solution)/shard_map/all_gather | solution.py:142
  405.9 8.6 fusion.28
  419.2 15.6 %fusion.21 = (bf16[4096]{0:T(1024)(128)(2,1)}, bf16[512,4096]{1,0:T(8,128)(2,1)}) fusion(f32[512,4096]{1,0:T(8,128)} %get-tuple-element.162, f32[512,4096]{1,0:T(8,128)} %get-tuple-element.168, f32[4096]{0:T(1024)S(1)} %bitcast.101, bf16[512,1024]{1,0:T(8,128)(2,1)S(1)} %get-tuple-element.152, bf16[4096,1024]{0,1:T(8,128)(2,1)} %all-gather.18.cloned.1.call-done), kind=kOutput, calls=%fused_computation.86 | convolution fusion | flops 4328517632 | bytes 30433280 | tf_op jit(solution)/shard_map/dot_general | solution.py:22
  448.8 14.4 %multiply_reduce_fusion = (f32[16,512]{1,0:T(8,128)}, f32[16,512,512]{1,2,0:T(8,128)}) fusion(f32[16,512,512]{1,2,0:T(8,128)} %get-tuple-element.165, f32[16,512]{1,0:T(8,128)} %log_add_fusion, bf16[512,16,64]{0,2,1:T(8,128)(2,1)S(1)} %bitcast.86, bf16[512,16,64]{0,2,1:T(8,128)(2,1)} %bitcast.89), kind=kOutput, calls=%fused_computation.1 | convolution fusion | flops 549445632 | bytes 35717120 | tf_op jit(solution)/shard_map/while/body/eval_jaxpr/qhe,khe->hqk/dot_general | solution.py:79
  495.9 9.4 fusion.30
  514.4 9.6 convolution_convert_fusion.1
  525.2 8.9 convolution_convert_fusion
  534.3 17.0 %reduce-scatter.37.cloned.1.call-done = bf16[128,1024]{1,0:T(8,128)(2,1)} async-done(((bf16[1024,1024]{1,0:T(8,128)(2,1)}), bf16[128,1024]{1,0:T(8,128)(2,1)}) %reduce-scatter.37.cloned.1.call-update) | async-done | bytes 262160
  551.4 70.2 %reduce-scatter.41.cloned.1.call-done = bf16[128,1024]{1,0:T(8,128)(2,1)} async-done(((bf16[1024,1024]{1,0:T(8,128)(2,1)}), bf16[128,1024]{1,0:T(8,128)(2,1)}) %reduce-scatter.41.cloned.1.call-update) | async-done | bytes 262160
  621.6 70.2 %reduce-scatter.45.cloned.1.call-done = bf16[128,1024]{1,0:T(8,128)(2,1)} async-done(((bf16[1024,1024]{1,0:T(8,128)(2,1)}), bf16[128,1024]{1,0:T(8,128)(2,1)}) %reduce-scatter.45.cloned.1.call-update) | async-done | bytes 262160
  691.9 69.9 %reduce-scatter.25.cloned.1.call-done = bf16[128,1024]{1,0:T(8,128)(2,1)} async-done(((bf16[1024,1024]{1,0:T(8,128)(2,1)}), bf16[128,1024]{1,0:T(8,128)(2,1)}) %reduce-scatter.25.cloned.1.call-update) | async-done | bytes 262160 | tf_op jit(solution)/shard_map/reduce_scatter | solution.py:249
  761.9 151.6 %reduce-scatter.29.cloned.1.call-done = bf16[128,4096]{1,0:T(8,128)(2,1)} async-done(((bf16[1024,4096]{1,0:T(8,128)(2,1)}), bf16[128,4096]{1,0:T(8,128)(2,1)}) %reduce-scatter.29.cloned.1.call-update) | async-done | bytes 1048592 | tf_op jit(solution)/shard_map/reduce_scatter | solution.py:252
  913.5 151.9 %reduce-scatter.33.cloned.1.call-done = bf16[128,4096]{1,0:T(8,128)(2,1)} async-done(((bf16[1024,4096]{1,0:T(8,128)(2,1)}), bf16[128,4096]{1,0:T(8,128)(2,1)}) %reduce-scatter.33.cloned.1.call-update) | async-done | bytes 1048592 | tf_op jit(solution)/shard_map/reduce_scatter | solution.py:255
  1069.5 35.2 %all-reduce.27 = (bf16[1024]{0:T(1024)(128)(2,1)S(1)}, bf16[1024]{0:T(1024)(128)(2,1)S(1)}, bf16[1024]{0:T(1024)(128)(2,1)S(1)}, bf16[4096]{0:T(1024)(128)(2,1)S...) all-reduce(bf16[1024]{0:T(1024)(128)(2,1)S(1)} %reduce_sum.235, ...), channel_id=14, replica_groups=mesh['dp'=8,'fsdp'=4] {'dp'}, use_global_device_ids=true, to_apply=%region_24.25.clone | all-reduce | flops 12288 | bytes 49152
  1133.8 20.7 %reduce-scatter.27.cloned.1.call-done = bf16[32,1024]{1,0:T(8,128)(2,1)} async-done(((bf16[128,1024]{1,0:T(8,128)(2,1)}), bf16[32,1024]{1,0:T(8,128)(2,1)}) %reduce-scatter.27.cloned.1.call-update) | async-done | bytes 65552 | tf_op jit(solution)/shard_map/reduce_scatter | solution.py:296
  1156.0 25.8 %reduce-scatter.31.cloned.1.call-done = bf16[32,4096]{1,0:T(8,128)(2,1)} async-done(((bf16[128,4096]{1,0:T(8,128)(2,1)}), bf16[32,4096]{1,0:T(8,128)(2,1)}) %reduce-scatter.31.cloned.1.call-update) | async-done | bytes 262160 | tf_op jit(solution)/shard_map/reduce_scatter | solution.py:299
  1183.6 25.7 %reduce-scatter.35.cloned.1.call-done = bf16[32,4096]{1,0:T(8,128)(2,1)} async-done(((bf16[128,4096]{1,0:T(8,128)(2,1)}), bf16[32,4096]{1,0:T(8,128)(2,1)}) %reduce-scatter.35.cloned.1.call-update) | async-done | bytes 262160 | tf_op jit(solution)/shard_map/reduce_scatter | solution.py:302
  (256 shorter events, 158.4 us)
Async XLA Ops:
  7.2 102.3 %all-gather.8.cloned.1.call-start = ((), (), s32[]{:S(2)}) async-start(), calls=%async_computation.12 | async-start | bytes 2162688 | tf_op jit(solution)/shard_map/all_gather | solution.py:131
  8.8 120.6 %all-gather.10.cloned.1.call-start = ((), (), s32[]{:S(2)}) async-start(), calls=%async_computation.13 | async-start | bytes 2162688 | tf_op jit(solution)/shard_map/all_gather | solution.py:129
  10.4 177.7 %all-gather.12.cloned.1.call-start = ((), (), s32[]{:S(2)}) async-start(), calls=%async_computation.14 | async-start | bytes 2162688 | tf_op jit(solution)/shard_map/all_gather | solution.py:130
  12.0 234.7 %all-gather.14.cloned.1.call-start = ((), (), s32[]{:S(2)}) async-start(), calls=%async_computation.15 | async-start | bytes 2162688 | tf_op jit(solution)/shard_map/all_gather | solution.py:132
  13.7 312.8 %all-gather.16.cloned.1.call-start = ((), (), s32[]{:S(2)}) async-start(), calls=%async_computation.16 | async-start | bytes 8650752 | tf_op jit(solution)/shard_map/all_gather | solution.py:141
  15.5 390.4 %all-gather.18.cloned.1.call-start = ((), (), s32[]{:S(2)}) async-start(), calls=%async_computation.17 | async-start | bytes 8650752 | tf_op jit(solution)/shard_map/all_gather | solution.py:142
  17.4 533.9 %reduce-scatter.37.cloned.1.call-start = ((), (), s32[]{:S(2)}) async-start(), calls=%async_computation.24 | async-start | bytes 2359296
  484.8 136.8 %reduce-scatter.41.cloned.1.call-start = ((), (), s32[]{:S(2)}) async-start(), calls=%async_computation.26 | async-start | bytes 2359296
  495.8 196.0 %reduce-scatter.45.cloned.1.call-start = ((), (), s32[]{:S(2)}) async-start(), calls=%async_computation.28 | async-start | bytes 2359296
  510.3 251.6 %reduce-scatter.25.cloned.1.call-start = ((), (), s32[]{:S(2)}) async-start(), calls=%async_computation.18 | async-start | bytes 2359296 | tf_op jit(solution)/shard_map/reduce_scatter | solution.py:249
  514.3 399.1 %reduce-scatter.29.cloned.1.call-start = ((), (), s32[]{:S(2)}) async-start(), calls=%async_computation.20 | async-start | bytes 9437184 | tf_op jit(solution)/shard_map/reduce_scatter | solution.py:252
  524.0 541.5 %reduce-scatter.33.cloned.1.call-start = ((), (), s32[]{:S(2)}) async-start(), calls=%async_computation.22 | async-start | bytes 9437184 | tf_op jit(solution)/shard_map/reduce_scatter | solution.py:255
  534.2 535.3 %copy-start.31 = (bf16[1024]{0:T(1024)(128)(2,1)S(1)}, bf16[1024]{0:T(1024)(128)(2,1)}, u32[]{:S(2)}) copy-start(bf16[1024]{0:T(1024)(128)(2,1)} %get-tuple-element.121) | copy-start | bytes 6148
  534.2 535.3 %copy-start.32 = (bf16[1024]{0:T(1024)(128)(2,1)S(1)}, bf16[1024]{0:T(1024)(128)(2,1)}, u32[]{:S(2)}) copy-start(bf16[1024]{0:T(1024)(128)(2,1)} %get-tuple-element.124) | copy-start | bytes 6148
  534.2 535.3 %copy-start.33 = (bf16[1024]{0:T(1024)(128)(2,1)S(1)}, bf16[1024]{0:T(1024)(128)(2,1)}, u32[]{:S(2)}) copy-start(bf16[1024]{0:T(1024)(128)(2,1)} %get-tuple-element.151) | copy-start | bytes 6148
  534.2 535.3 %copy-start.34 = (bf16[1024]{0:T(1024)(128)(2,1)S(1)}, bf16[1024]{0:T(1024)(128)(2,1)}, u32[]{:S(2)}) copy-start(bf16[1024]{0:T(1024)(128)(2,1)} %get-tuple-element.155) | copy-start | bytes 6148
  534.2 535.3 %copy-start.37 = (bf16[4096]{0:T(1024)(128)(2,1)S(1)}, bf16[4096]{0:T(1024)(128)(2,1)}, u32[]{:S(2)}) copy-start(bf16[4096]{0:T(1024)(128)(2,1)} %get-tuple-element.153) | copy-start | bytes 24580
  534.2 579.8 %copy-start.18 = (bf16[16,64,512]{2,1,0:T(8,128)(2,1)S(1)}, bf16[16,64,512]{2,1,0:T(8,128)(2,1)}, u32[]{:S(2)}) copy-start(bf16[16,64,512]{2,1,0:T(8,128)(2,1)} %copy-done.17) | copy-start | bytes 3145732
  534.3 588.3 %reduce-scatter.39.cloned.1.call-start = ((), (), s32[]{:S(2)}) async-start(), calls=%async_computation.25 | async-start | bytes 327680
  551.3 573.1 %reduce-scatter.43.cloned.1.call-start = ((), (), s32[]{:S(2)}) async-start(), calls=%async_computation.27 | async-start | bytes 327680
  621.6 510.4 %reduce-scatter.47.cloned.1.call-start = ((), (), s32[]{:S(2)}) async-start(), calls=%async_computation.29 | async-start | bytes 327680
  691.9 462.6 %reduce-scatter.27.cloned.1.call-start = ((), (), s32[]{:S(2)}) async-start(), calls=%async_computation.19 | async-start | bytes 327680 | tf_op jit(solution)/shard_map/reduce_scatter | solution.py:296
  761.9 419.9 %reduce-scatter.31.cloned.1.call-start = ((), (), s32[]{:S(2)}) async-start(), calls=%async_computation.21 | async-start | bytes 1310720 | tf_op jit(solution)/shard_map/reduce_scatter | solution.py:299
  913.5 295.7 %reduce-scatter.35.cloned.1.call-start = ((), (), s32[]{:S(2)}) async-start(), calls=%async_computation.23 | async-start | bytes 1310720 | tf_op jit(solution)/shard_map/reduce_scatter | solution.py:302
  (45 other events, 4074.6 us)
Sparse Core Ops, SparseCore 0:
  11.5 59.2 all-gather.7
  74.1 55.2 all-gather.9
  132.9 55.2 all-gather.11
  191.4 55.2 all-gather.13
  250.0 76.4 all-gather.15
  329.8 76.1 all-gather.17
  484.9 66.3 reduce-scatter.36
  554.8 66.7 reduce-scatter.40
  625.1 66.6 reduce-scatter.44
  695.2 66.5 reduce-scatter.24
  765.5 147.9 reduce-scatter.28
  917.4 148.0 reduce-scatter.32
  1067.9 19.0 reduce-scatter.38
  1089.5 19.9 reduce-scatter.42
  1111.8 20.1 reduce-scatter.46
  1134.4 19.9 reduce-scatter.26
  1156.8 24.9 reduce-scatter.30
  1184.3 24.8 reduce-scatter.34
where the time goes:
time: 1220 us
  waiting for transfers between devices  836 us (69%)
  matrix products  157 us (13%)
  blocking collectives  124 us (10%)
  other arithmetic  49.4 us (4%)
  local copies, waits for them, and re-layouts  33.4 us (3%)
  between operations  18.1 us (1%)
    unnamed x24, waiting for transfers between devices  163 us
    reduce_scatter x1, waiting for transfers between devices, per_device(): lax.psum_scatter(members[5].astype(jnp.bfloat16), 'dp', scatter_dimension...  152 us
    reduce_scatter x1, waiting for transfers between devices, per_device(): lax.psum_scatter(members[4].astype(jnp.bfloat16), 'dp', scatter_dimension...  152 us
    unnamed x3, blocking collectives  83.3 us
    all_gather x1, waiting for transfers between devices, per_device(): lax.all_gather(to_half(up_w), ('dp', 'fsdp'), axis=0, tiled=True)  74.9 us
    reduce_scatter x1, waiting for transfers between devices, per_device(): lax.psum_scatter(members[3].astype(jnp.bfloat16), 'dp', scatter_dimension...  69.9 us
    all_gather x1, waiting for transfers between devices, per_device(): lax.all_gather(to_half(key_w), ('dp', 'fsdp'), axis=0, tiled=True)  55.3 us
    all_gather x1, waiting for transfers between devices, per_device(): lax.all_gather(to_half(down_w), ('dp', 'fsdp'), axis=1, tiled=True)  51.6 us
  transfers between devices with their start and end apart: 18, of which 15 were waited for; matrix products, arithmetic and copies ran while one was open for 13% of the time, Pallas kernels for 0%

commit v1 on v0

--- a/solution.py
+++ b/solution.py
@@ -1,7 +1,314 @@
+import functools
+
 import jax
 import jax.numpy as jnp
 from jax import lax
+from jax.experimental import pallas as pl
+from jax.experimental.pallas import tpu as pltpu
 from jax.sharding import PartitionSpec as P
+
+MESH = pl.DeviceIdType.MESH
+BLOCKS = 12
+
+
+def place():
+    dp = lax.axis_index("dp")
+    fs = lax.axis_index("fsdp")
+    return dp // 2, dp % 2, fs // 2, fs % 2
+
+
+def device(z, x, y, c):
+    return (z * 2 + x, y * 2 + c)
+
+
+def greet(depth):
+    z, x, y, c = place()
+    peers = [device(z, x, y, 1 - c), device(z, 1 - x, y, c), device(z, x, 1 - y, c)]
+    peers += [device((z + k) % depth, x, y, c) for k in range(1, depth)]
+    bar = pltpu.get_barrier_semaphore()
+    for peer in peers:
+        pl.semaphore_signal(bar, inc=1, device_id=peer, device_id_type=MESH)
+    pl.semaphore_wait(bar, len(peers))
+
+
+def send(src, dst, ssem, rsem, peer):
+    return pltpu.make_async_remote_copy(
+        src_ref=src, dst_ref=dst, send_sem=ssem, recv_sem=rsem, device_id=peer, device_id_type=MESH
+    )
+
+
+class GatherBlock:
+    def __init__(self, full, mine, ss, rs, depth):
+        self.full, self.ss, self.rs, self.depth = full, ss, rs, depth
+        self.mine = mine
+        z, x, y, c = self.at = place()
+        self.xn, self.yn, self.cn = device(z, 1 - x, y, c), device(z, x, 1 - y, c), device(z, x, y, 1 - c)
+        half = depth // 2
+        self.low, self.high = pl.ds(0, half), pl.ds(half, depth - half)
+
+    def moves(self):
+        z, x, y, c = self.at
+        full, ss, rs = self.full, self.ss, self.rs
+        every = pl.ds(0, self.depth)
+        out = {}
+        own = full.at[z, x, y, c]
+        for k in range(1, self.depth):
+            out["col", k] = send(own, own, ss.at[k - 1], rs.at[k - 1], device((z + k) % self.depth, x, y, c))
+        base = self.depth - 1
+        column = full.at[every, x, y, c]
+        out["x"] = send(column, column, ss.at[base], rs.at[base], self.xn)
+        out["y"] = send(column, column, ss.at[base + 1], rs.at[base + 1], self.yn)
+        out["c0"] = send(column, column, ss.at[base + 2], rs.at[base + 2], self.cn)
+        xcol = full.at[every, 1 - x, y, c]
+        ycol = full.at[every, x, 1 - y, c]
+        out["c1"] = send(xcol, xcol, ss.at[base + 3], rs.at[base + 3], self.cn)
+        out["c2"] = send(ycol, ycol, ss.at[base + 4], rs.at[base + 4], self.cn)
+        xlow = full.at[self.low, 1 - x, y, c]
+        yhigh = full.at[self.high, x, 1 - y, c]
+        out["dy"] = send(xlow, xlow, ss.at[base + 5], rs.at[base + 5], self.yn)
+        out["dx"] = send(yhigh, yhigh, ss.at[base + 6], rs.at[base + 6], self.xn)
+        dcol = full.at[every, 1 - x, 1 - y, c]
+        out["c3"] = send(dcol, dcol, ss.at[base + 7], rs.at[base + 7], self.cn)
+        return out
+
+    def arrivals(self):
+        z, x, y, c = self.at
+        full, ss, rs = self.full, self.ss, self.rs
+        every = pl.ds(0, self.depth)
+        out = {}
+
+        def got(ref, i):
+            return send(ref, ref, ss.at[i], rs.at[i], self.cn)
+
+        for k in range(1, self.depth):
+            out["col", k] = got(full.at[(z + self.depth - k) % self.depth, x, y, c], k - 1)
+        base = self.depth - 1
+        out["x"] = got(full.at[every, 1 - x, y, c], base)
+        out["y"] = got(full.at[every, x, 1 - y, c], base + 1)
+        out["c0"] = got(full.at[every, x, y, 1 - c], base + 2)
+        out["c1"] = got(full.at[every, 1 - x, y, 1 - c], base + 3)
+        out["c2"] = got(full.at[every, x, 1 - y, 1 - c], base + 4)
+        out["dy"] = got(full.at[self.low, 1 - x, 1 - y, c], base + 5)
+        out["dx"] = got(full.at[self.high, 1 - x, 1 - y, c], base + 6)
+        out["c3"] = got(full.at[every, 1 - x, 1 - y, 1 - c], base + 7)
+        return out
+
+    def stage(self, s):
+        moves, arrivals = self.moves(), self.arrivals()
+        if s == 0:
+            z, x, y, c = self.at
+            self.full[z, x, y, c] = self.mine[...]
+            for k in range(1, self.depth):
+                moves["col", k].start()
+        if s == 1:
+            for k in range(1, self.depth):
+                arrivals["col", k].wait_recv()
+            for name in ("x", "y", "c0"):
+                moves[name].start()
+        if s == 2:
+            arrivals["x"].wait_recv()
+            moves["dy"].start()
+            moves["c1"].start()
+            arrivals["y"].wait_recv()
+            moves["dx"].start()
+            moves["c2"].start()
+        if s == 3:
+            arrivals["dy"].wait_recv()
+            arrivals["dx"].wait_recv()
+            moves["c3"].start()
+        if s == 4:
+            for name in ("c0", "c1", "c2", "c3"):
+                arrivals[name].wait_recv()
+            for move in moves.values():
+                move.wait_send()
+
+
+def gather_kernel(depth, shard_ref, vec_ref, wout_ref, vout_ref, full, vfull, ss, rs, osem):
+    greet(depth)
+
+    def block(b):
+        return GatherBlock(full.at[b], shard_ref.at[b], ss.at[b], rs.at[b], depth)
+
+    vec = GatherBlock(vfull, vec_ref, ss.at[BLOCKS], rs.at[BLOCKS], depth)
+    for t in range(BLOCKS + 4):
+        for s in range(5):
+            b = t - s
+            if 0 <= b < BLOCKS:
+                block(b).stage(s)
+                if s == 4:
+                    pltpu.make_async_copy(full.at[b], wout_ref.at[b], osem.at[b]).start()
+            if b == 1:
+                vec.stage(s)
+    vout_ref[...] = vfull[...]
+    for b in range(BLOCKS):
+        pltpu.make_async_copy(full.at[b], wout_ref.at[b], osem.at[b]).wait()
+
+
+def gather_call(shard, vec, depth):
+    rows, cols = shard.shape[1:]
+    dims = (depth, 2, 2, 2)
+    n = depth + 7
+    return pl.pallas_call(
+        functools.partial(gather_kernel, depth),
+        out_shape=(
+            jax.ShapeDtypeStruct((BLOCKS,) + dims + (rows, cols), jnp.bfloat16),
+            jax.ShapeDtypeStruct(dims + vec.shape, jnp.bfloat16),
+        ),
+        in_specs=[pl.BlockSpec(memory_space=pltpu.VMEM)] * 2,
+        out_specs=(pl.BlockSpec(memory_space=pl.ANY), pl.BlockSpec(memory_space=pltpu.VMEM)),
+        scratch_shapes=[
+            pltpu.VMEM((BLOCKS,) + dims + (rows, cols), jnp.bfloat16),
+            pltpu.VMEM(dims + vec.shape, jnp.bfloat16),
+            pltpu.SemaphoreType.DMA((BLOCKS + 1, n)),
+            pltpu.SemaphoreType.DMA((BLOCKS + 1, n)),
+            pltpu.SemaphoreType.DMA((BLOCKS,)),
+        ],
+        compiler_params=pltpu.CompilerParams(
+            collective_id=0, has_side_effects=True, vmem_limit_bytes=56 * 2**20
+        ),
+        name="gather",
+    )(shard, vec)
+
+
+class SumBlock:
+    def __init__(self, grad, r0, r1x, r1y, r2x, r2y, r3, ss, rs, depth):
+        self.grad, self.r0, self.r1x, self.r1y, self.r2x, self.r2y, self.r3 = grad, r0, r1x, r1y, r2x, r2y, r3
+        self.ss, self.rs, self.depth = ss, rs, depth
+        self.at = place()
+
+    def moves(self):
+        z, x, y, c = self.at
+        xn, yn, cn = device(z, 1 - x, y, c), device(z, x, 1 - y, c), device(z, x, y, 1 - c)
+        g, ss, rs, depth = self.grad, self.ss, self.rs, self.depth
+        half = depth // 2
+        low, high, every = pl.ds(0, half), pl.ds(half, depth - half), pl.ds(0, depth)
+        out = {}
+        out["c"] = send(g.at[every, pl.ds(0, 2), pl.ds(0, 2), 1 - c], self.r0, ss.at[0], rs.at[0], cn)
+        out["dx"] = send(g.at[low, 1 - x, 1 - y, c], self.r1x, ss.at[1], rs.at[1], xn)
+        out["dy"] = send(g.at[high, 1 - x, 1 - y, c], self.r1y, ss.at[2], rs.at[2], yn)
+        out["x"] = send(g.at[every, 1 - x, y, c], self.r2x, ss.at[3], rs.at[3], xn)
+        out["y"] = send(g.at[every, x, 1 - y, c], self.r2y, ss.at[4], rs.at[4], yn)
+        for k in range(1, depth):
+            out["z", k] = send(
+                g.at[(z + k) % depth, x, y, c], self.r3.at[k - 1], ss.at[4 + k], rs.at[4 + k],
+                device((z + k) % depth, x, y, c),
+            )
+        return out
+
+    def stage(self, s, out=None):
+        m = self.moves()
+        z, x, y, c = self.at
+        g, depth = self.grad, self.depth
+        half = depth // 2
+        if s == 0:
+            m["c"].start()
+        if s == 1:
+            m["c"].wait_recv()
+            for xx, yy in ((1 - x, 1 - y), (1 - x, y), (x, 1 - y), (x, y)):
+                for zz in range(depth):
+                    g[zz, xx, yy, c] = g[zz, xx, yy, c] + self.r0[zz, xx, yy]
+                if xx is not x and yy is not y:
+                    m["dx"].start()
+                    m["dy"].start()
+        if s == 2:
+            m["dx"].wait_recv()
+            for zz in range(half):
+                g[zz, x, 1 - y, c] = g[zz, x, 1 - y, c] + self.r1x[zz]
+            m["y"].start()
+            m["dy"].wait_recv()
+            for zz in range(half, depth):
+                g[zz, 1 - x, y, c] = g[zz, 1 - x, y, c] + self.r1y[zz - half]
+            m["x"].start()
+        if s == 3:
+            m["x"].wait_recv()
+            m["y"].wait_recv()
+            for k in list(range(1, depth)) + [0]:
+                zz = (z + k) % depth
+                total = (
+                    g[zz, x, y, c].astype(jnp.float32)
+                    + self.r2x[zz].astype(jnp.float32)
+                    + self.r2y[zz].astype(jnp.float32)
+                )
+                g[zz, x, y, c] = total.astype(jnp.bfloat16)
+                if k:
+                    m["z", k].start()
+        if s == 4:
+            total = g[z, x, y, c].astype(jnp.float32)
+            for k in range(1, depth):
+                m["z", k].wait_recv()
+                total = total + self.r3[k - 1].astype(jnp.float32)
+            out[...] = total
+            for move in m.values():
+                move.wait_send()
+
+
+SLOTS = 6
+
+
+def sum_scratch(depth, rows, cols, slots, n_sems):
+    bf = jnp.bfloat16
+    half = depth // 2
+    return [
+        pltpu.VMEM((slots, depth, 2, 2, 2, rows, cols), bf),
+        pltpu.VMEM((slots, depth, 2, 2, rows, cols), bf),
+        pltpu.VMEM((slots, half, rows, cols), bf),
+        pltpu.VMEM((slots, depth - half, rows, cols), bf),
+        pltpu.VMEM((slots, depth, rows, cols), bf),
+        pltpu.VMEM((slots, depth, rows, cols), bf),
+        pltpu.VMEM((slots, depth - 1, rows, cols), bf),
+        pltpu.SemaphoreType.DMA((n_sems, depth + 4)),
+        pltpu.SemaphoreType.DMA((n_sems, depth + 4)),
+    ]
+
+
+def sum_kernel(depth, grads_ref, vgrad_ref, out_ref, vout_ref, *scratch):
+    big, vec, lsem = scratch[:9], scratch[9:18], scratch[18]
+    greet(depth)
+
+    def block(b):
+        slot = b % SLOTS
+        return SumBlock(*[r.at[slot] for r in big[:7]], big[7].at[b], big[8].at[b], depth)
+
+    vblock = SumBlock(*[r.at[0] for r in vec[:7]], vec[7].at[0], vec[8].at[0], depth)
+
+    def fetch(b):
+        return pltpu.make_async_copy(grads_ref.at[b], big[0].at[b % SLOTS], lsem.at[b])
+
+    vec[0][0] = vgrad_ref[...]
+    fetch(0).start()
+    for t in range(BLOCKS + 4):
+        if t < BLOCKS:
+            if t + 1 < BLOCKS:
+                fetch(t + 1).start()
+            fetch(t).wait()
+        for s in range(5):
+            b = t - s
+            if 0 <= b < BLOCKS:
+                block(b).stage(s, out_ref.at[b])
+            if b == 1:
+                vblock.stage(s, vout_ref)
+
+
+def sum_call(grads, vgrad, depth):
+    rows, cols = grads.shape[-2:]
+    vrows, vcols = vgrad.shape[-2:]
+    return pl.pallas_call(
+        functools.partial(sum_kernel, depth),
+        out_shape=(
+            jax.ShapeDtypeStruct((BLOCKS, rows, cols), jnp.float32),
+            jax.ShapeDtypeStruct((vrows, vcols), jnp.float32),
+        ),
+        in_specs=[pl.BlockSpec(memory_space=pl.ANY), pl.BlockSpec(memory_space=pltpu.VMEM)],
+        out_specs=(pl.BlockSpec(memory_space=pltpu.VMEM),) * 2,
+        scratch_shapes=sum_scratch(depth, rows, cols, SLOTS, BLOCKS)
+        + sum_scratch(depth, vrows, vcols, 1, 1)
+        + [pltpu.SemaphoreType.DMA((BLOCKS,))],
+        compiler_params=pltpu.CompilerParams(
+            collective_id=1, has_side_effects=True, vmem_limit_bytes=56 * 2**20
+        ),
+        name="sum_grads",
+    )(grads, vgrad)
+
 
 HEAD = 64
 
@@ -98,7 +405,7 @@
     )
 
 
-def per_device(
+def plain_device(
     tokens,
     segment,
     cotangent,
@@ -369,7 +676,118 @@
     )
 
 
+def kernel_device(
+    tokens, segment, cotangent, query_w, key_w, value_w, attn_out_w, up_w, down_w, query_bias, value_bias,
+    attn_out_bias, up_bias, down_bias, norm1_gain, norm1_shift, norm2_gain, norm2_shift,
+):
+    row_count, row_length = segment.shape
+    model_width = tokens.shape[1]
+    depth = lax.axis_size("dp") // 2
+    fs = lax.axis_index("fsdp")
+    rows = query_w.shape[0]
+    quarters = up_w.shape[1] // model_width
+
+    def by_rows(array):
+        return array.reshape(row_count, row_length, -1)
+
+    def quarter(array):
+        return [array[:, i * model_width : (i + 1) * model_width] for i in range(quarters)]
+
+    down_turned = jnp.transpose(to_half(down_w))
+    shard = jnp.stack(
+        [to_half(w) for w in (query_w, key_w, value_w, attn_out_w)] + quarter(to_half(up_w)) + quarter(down_turned)
+    )
+    short = jnp.stack(
+        [query_bias, value_bias, attn_out_bias, down_bias, norm1_gain, norm1_shift, norm2_gain, norm2_shift]
+    )
+    at_lane = jnp.arange(128)[None, :] // rows == fs
+    short = jnp.where(at_lane, jnp.tile(short, (1, 128 // rows)), 0.0)
+    at_row = jnp.arange(8)[:, None] == fs
+    tile = to_half(jnp.concatenate([short, jnp.where(at_row, up_bias[None], 0.0)]))
+
+    full, vectors = gather_call(shard, tile, depth)
+    full = full.reshape(BLOCKS, model_width, model_width)
+    vectors = vectors.reshape(2 * depth, 4, 16, 128).astype(jnp.float32).sum(axis=1)
+    short_full = jnp.moveaxis(vectors[:, :8], 0, 1).reshape(8, model_width)
+    bias_q, bias_v, bias_o, bias_down, gain_one, shift_one, gain_two, shift_two = short_full
+    bias_up = vectors[:, 8:12].reshape(-1)
+    wq_full, wk_full, wv_full, wo_full = [full[i] for i in range(4)]
+    ups, downs = full[4:8], full[8:12]
+
+    queries = to_half(matmul(tokens, wq_full) + bias_q)
+    key_rows = to_half(matmul(tokens, wk_full))
+    value_rows = to_half(matmul(tokens, wv_full) + bias_v)
+    context, log_total = lax.map(
+        attend_row, (by_rows(queries), by_rows(key_rows), by_rows(value_rows), segment)
+    )
+    context = context.reshape(-1, model_width)
+    attended = matmul(context, wo_full) + bias_o
+    first_sum = tokens.astype(jnp.float32) + attended
+    norm_mid, pull_one = jax.vjp(normalize, first_sum, gain_one, shift_one)
+    mid_half = to_half(norm_mid)
+    pre_act = jnp.concatenate([matmul(mid_half, w) for w in ups], axis=1) + bias_up
+    act_out, pull_act = jax.vjp(gelu_exact, pre_act)
+    act_half = to_half(act_out)
+    ffn_out = sum(matmul_nt(a, w) for a, w in zip(quarter(act_half), downs)) + bias_down
+    second_sum = mid_half.astype(jnp.float32) + ffn_out
+    final, pull_two = jax.vjp(normalize, second_sum, gain_two, shift_two)
+    outputs = to_half(final)
+    valid = (segment.reshape(-1) >= 0).astype(jnp.float32)[:, None]
+    d_out = cotangent.astype(jnp.float32) * valid
+    d_second, d_gain_two, d_shift_two = pull_two(d_out)
+    d_ffn = to_half(d_second)
+    d_down_turned = [contract_rows(d_ffn, a) for a in quarter(act_half)]
+    d_down_bias = column_sums(d_ffn)
+    (d_pre,) = pull_act(jnp.concatenate([matmul(d_ffn, w) for w in downs], axis=1))
+    d_pre_half = to_half(d_pre)
+    d_up_w = [contract_rows(mid_half, d) for d in quarter(d_pre_half)]
+    d_up_bias = column_sums(d_pre_half)
+    d_mid = d_second + sum(matmul_nt(d, w) for d, w in zip(quarter(d_pre_half), ups))
+    d_first, d_gain_one, d_shift_one = pull_one(d_mid)
+    d_att = to_half(d_first)
+    d_attn_out_w = contract_rows(context, d_att)
+    d_attn_out_bias = column_sums(d_att)
+    d_context = to_half(matmul_nt(d_att, wo_full))
+    d_queries, d_keys, d_values = lax.map(
+        attend_back,
+        (by_rows(queries), by_rows(key_rows), by_rows(value_rows), segment, log_total, by_rows(d_context)),
+    )
+    d_queries = d_queries.reshape(-1, model_width)
+    d_keys = d_keys.reshape(-1, model_width)
+    d_values = d_values.reshape(-1, model_width)
+    d_query_w = contract_rows(tokens, d_queries)
+    d_key_w = contract_rows(tokens, d_keys)
+    d_value_w = contract_rows(tokens, d_values)
+    d_tokens = (
+        d_first + matmul_nt(d_queries, wq_full) + matmul_nt(d_keys, wk_full) + matmul_nt(d_values, wv_full)
+    )
+    grads = [to_half(g) for g in d_down_turned + d_up_w + [d_attn_out_w, d_value_w, d_key_w, d_query_w]]
+    grads = jnp.stack(grads).reshape(BLOCKS, depth, 2, 2, 2, rows, model_width)
+    short_grads = jnp.stack(
+        [
+            column_sums(d_queries), column_sums(d_values), d_attn_out_bias, d_down_bias,
+            d_gain_one, d_shift_one, d_gain_two, d_shift_two,
+        ]
+    )
+    short_grads = jnp.moveaxis(short_grads.reshape(8, 2 * depth, 1, 128), 0, 2)
+    short_grads = jnp.broadcast_to(short_grads, (2 * depth, 4, 8, 128))
+    up_grads = d_up_bias.reshape(2 * depth, 4, 1, 128)
+    up_grads = jnp.broadcast_to(up_grads, (2 * depth, 4, 8, 128))
+    tiles = to_half(jnp.concatenate([short_grads, up_grads], axis=2)).reshape(depth, 2, 2, 2, 16, 128)
+    sums, tile_sum = sum_call(grads, tiles, depth)
+    short_sum = lax.dynamic_slice(tile_sum, (0, fs * rows), (8, rows))
+    qb, vb, ob, db, g1, s1, g2, s2 = short_sum
+    ub = tile_sum[8]
+    dw = jnp.transpose(jnp.concatenate(list(sums[:4]), axis=1))
+    uw = jnp.concatenate(list(sums[4:8]), axis=1)
+    return (
+        outputs, d_tokens, sums[11], sums[10], sums[9], sums[8], uw, dw, qb, vb, ob, ub, db, g1, s1, g2, s2,
+    )
+
+
 def solution(mesh):
+    fits = mesh.shape["fsdp"] == 4 and mesh.shape["dp"] % 2 == 0 and 1024 // mesh.size == 32
+    body = kernel_device if fits else plain_device
     in_specs = (
         P(("dp", "fsdp"), None),
         P(("dp", "fsdp"), None),
@@ -410,5 +828,5 @@
         P(("dp", "fsdp")),
     )
     return jax.shard_map(
-        per_device, mesh=mesh, in_specs=in_specs, out_specs=out_specs, check_vma=False
-    )
+        body, mesh=mesh, in_specs=in_specs, out_specs=out_specs, check_vma=False
+    )

time: 1220 us -> 492 us (0.40)
  waiting for transfers between devices: 836 us -> 0 us
  Pallas kernels: 0 us -> 246 us
  blocking collectives: 124 us -> 0 us
  matrix products: 157 us -> 122 us
  local copies, waits for them, and re-layouts: 33.4 us -> 57.6 us
  between operations: 18.1 us -> 1.65 us
    reduce_scatter x6 -> x0, waiting for transfers between devices: 446 us -> none  [the longest x1 152 us: per_device(): lax.psum_scatter(members[5].astype(jnp.bfloat16), 'dp', scatter_dimension...]
    pallas_call x0 -> x2, Pallas kernels: none -> 246 us  [the longest x1 123 us: sum_call(): pl.pallas_call(functools.partial(sum_kernel, depth), out_shape=(jax.Shape...]
    all_gather x6 -> x0, waiting for transfers between devices: 227 us -> none  [the longest x1 74.9 us: per_device(): lax.all_gather(to_half(up_w), ('dp', 'fsdp'), axis=0, tiled=True)]
    unnamed x24 -> x0, waiting for transfers between devices: 163 us -> none
    unnamed x3 -> x0, blocking collectives: 83.3 us -> none
    all_gather x1 -> x0, blocking collectives: 40.3 us -> none  [per_device(): lax.all_gather(to_half(up_bias), ('dp', 'fsdp'), axis=0, tiled=True)]
    dot_general x6 -> x12, matrix products: 50.2 us -> 22.4 us  [matmul(): return jnp.dot(left, right, preferred_element_type=jnp.float32)]
    another operation x0 -> x12, local copies, waits for them, and re-layouts: none -> 23.3 us  [the longest x1 17 us: kernel_device(): zip(quarter(act_half), downs)]
  transfers between devices with their start and end apart: 18 -> 0, of which waited for: 15 -> 0; matrix products, arithmetic and copies ran while one was open for 13% -> 0% of each run, Pallas kernels for 0% -> 0%
where the time goes in v1:
time: 492 us; the launch traced here: 488 us
  Pallas kernels  246 us (50%)
  matrix products  122 us (25%)
  other arithmetic  60.3 us (12%)
  local copies, waits for them, and re-layouts  57.6 us (12%)
    pallas_call x1, Pallas kernels, sum_call(): pl.pallas_call(functools.partial(sum_kernel, depth), out_shape=(jax.Shape...  123 us
    pallas_call x1, Pallas kernels, gather_call(): pl.pallas_call(functools.partial(gather_kernel, depth), out_shape=(jax.Sh...  123 us
    unnamed x152, local copies, waits for them, and re-layouts  32.1 us
    convert_element_type x4, other arithmetic, to_half(): return array.astype(jnp.bfloat16)  30.7 us
    dot_general x12, matrix products, contract_rows(): lax.dot_general(left, right, (((0,), (0,)), ((), ())), preferred_element_...  30.2 us
    dot_general x12, matrix products, matmul_nt(): lax.dot_general(left, right, (((1,), (1,)), ((), ())), preferred_element_...  27.7 us
    dot_general x12, matrix products, matmul(): return jnp.dot(left, right, preferred_element_type=jnp.float32)  22.4 us
    another operation x1, local copies, waits for them, and re-layouts, kernel_device(): zip(quarter(act_half), downs)  17 us

profile of v1, /device:TPU:0, one launch (start us, length us, event | category | flops | bytes accessed | tf_op | source)
XLA Modules:
  0.0 487.9 jit_solution(9819731070687047220)
XLA Ops:
  8.8 122.9 %gather.1 = (bf16[12,4,2,2,2,32,1024]{6,5,4,3,2,1,0:T(8,128)(2,1)}, bf16[4,2,2,2,16,128]{5,4,3,2,1,0:T(8,128)(2,1)}) custom-call(bf16[12,32,1024]{2,1,0:T(8,128)(2,1)} %copy-done.50, bf16[16,128]{1,0:T(8,128)(2,1)} %pad_maximum_fusion.3.vec_ref), custom_call_target="tpu_custom_call" | custom-call | tf_op jit(solution)/shard_map/gather/pallas_call | solution.py:151
  131.8 17.0 %fusion.55 = (bf16[1,4,2,2,2,32,1024]{6,5,4,3,2,1,0:T(8,128)(2,1)}, bf16[1,4,2,2,2,32,1024]{6,5,4,3,2,1,0:T(8,128)(2,1)}, bf16[1,4,2,2,2,32,1024]{6,5,4,3,2,1,0:...) fusion(bf16[12,4,2,2,2,32,1024]{6,5,4,3,2,1,0:T(8,128)(2,1)} %g, ...), kind=kLoop, calls=%fused_computation.180 | loop fusion | bytes 50331648 | tf_op jit(solution)/shard_map/unstack | solution.py:731
  148.9 3.0 add_convert_fusion.3
  155.2 7.4 %fusion.57 = (f32[16,512]{1,0:T(8,128)S(1)}, f32[16,512,512]{1,2,0:T(8,128)}) fusion(bf16[512,16,64]{0,2,1:T(8,128)(2,1)S(1)} %bitcast.251, bf16[512,16,64]{0,2,1:T(8,128)(2,1)S(1)} %bitcast.249, pred[512,512]{0,1:T(8,128)(4,1)S(1)} %broadcast_compare_fusion), kind=kOutput, calls=%fused_computation.182 | convolution fusion | flops 549445632 | bytes 19169280 | tf_op jit(solution)/shard_map/while/body/eval_jaxpr/qhe,khe->hqk/dot_general | solution.py:360
  162.7 8.3 %fusion = f32[16,512]{1,0:T(8,128)S(1)} fusion(f32[16,512,512]{1,2,0:T(8,128)} %get-tuple-element.136, f32[16,512]{1,0:T(8,128)S(1)} %get-tuple-element.135), kind=kLoop, calls=%fused_computation.6 | loop fusion | flops 8380416 | bytes 16842752 | tf_op jit(solution)/shard_map/while/body/eval_jaxpr/reduce_sum | solution.py:371
  171.0 7.9 %fusion.14 = bf16[16,64,512]{2,1,0:T(8,128)(2,1)S(1)} fusion(bf16[512,16,64]{0,2,1:T(8,128)(2,1)S(1)} %bitcast.285, f32[16,512,512]{1,2,0:T(8,128)} %get-tuple-element.136, f32[16,512]{1,0:T(8,128)S(1)} %fusion, f32[16,512]{1,0:T(8,128)S(1)} %get-tuple-element.135), kind=kOutput, calls=%fused_computation.69 | convolution fusion | flops 549978112 | bytes 18939904 | tf_op jit(solution)/shard_map/while/body/eval_jaxpr/hqk,khe->qhe/dot_general | solution.py:373
  187.5 18.6 %multiply_convert_fusion.1 = (bf16[512,4096]{1,0:T(8,128)(2,1)S(1)}, f32[512,4096]{1,0:T(8,128)S(1)}) fusion(f32[4096]{0:T(1024)S(1)} %bitcast.293, f32[512,1024]{1,0:T(8,128)S(1)} %fusion.63, f32[512,1024]{1,0:T(8,128)S(1)} %fusion.62, f32[512,1024]{1,0:T(8,128)S(1)} %fusion.61, f32[512,1024]{1,0:T(8,128)S(1)} %fusion.60), kind=kLoop, calls=%fused_computation.15 | loop fusion | flops 144703488 | bytes 20987904 | tf_op jit(solution)/shard_map/convert_element_type | solution.py:321
  206.1 2.6 fusion.32
  209.2 2.7 fusion.35
  211.9 2.7 fusion.38
  214.6 4.5 fusion.59
  234.5 7.9 %fusion.51 = (bf16[4096]{0:T(1024)(128)(2,1)S(1)}, bf16[512,4096]{1,0:T(8,128)(2,1)}) fusion(f32[512,4096]{1,0:T(8,128)S(1)} %get-tuple-element.93, f32[512,1024]{1,0:T(8,128)} %fusion.67, f32[512,1024]{1,0:T(8,128)} %fusion.66, f32[512,1024]{1,0:T(8,128)} %fusion.65, f32[512,1024]{1,0:T(8,128)} %fusion.64, f32[4096]{0:T(1024)S(1)} %bitcast.294, ...), kind=kLoop, calls=%fused_computation.177 | loop fusion | flops 46133248 | bytes 29384704 | tf_op jit(solution)/shard_map/reduce_sum | solution.py:341
  242.4 3.3 fusion.21
  256.2 3.8 convolution_convert_fusion.3
  260.0 8.7 %convert_reduce_fusion.2 = (bf16[16,64]{1,0:T(8,128)(2,1)S(1)}, bf16[16,64,512]{2,1,0:T(8,128)(2,1)S(1)}) fusion(bf16[512,16,64]{0,2,1:T(8,128)(2,1)S(1)} %bitcast.239, f32[16,512,512]{1,2,0:T(8,128)} %get-tuple-element.136, f32[16,512]{1,0:T(8,128)S(1)} %log_add_fusion), kind=kOutput, calls=%fused_computation.36 | convolution fusion | flops 546831360 | bytes 18909184 | tf_op jit(solution)/shard_map/while/body/eval_jaxpr/hqk,qhe->khe/dot_general | solution.py:398
  272.6 2.7 convolution_convert_fusion.6
  277.9 2.7 convolution_convert_fusion.4
  280.5 2.7 convolution_convert_fusion.7
  288.9 2.8 convolution_convert_fusion.10
  294.3 9.8 %multiply_reduce_fusion = (f32[16,512]{1,0:T(8,128)}, f32[16,512,512]{1,2,0:T(8,128)}) fusion(f32[16,512,512]{1,2,0:T(8,128)S(1)} %bitcast.238, f32[16,512]{1,0:T(8,128)} %copy-done.51, bf16[512,16,64]{0,2,1:T(8,128)(2,1)S(1)} %bitcast.240, bf16[512,16,64]{0,2,1:T(8,128)(2,1)} %bitcast.286), kind=kOutput, calls=%fused_computation.1 | convolution fusion | flops 549445632 | bytes 35717120 | tf_op jit(solution)/shard_map/while/body/eval_jaxpr/qhe,khe->hqk/dot_general | solution.py:386
  304.1 10.6 %multiply_convert_fusion = bf16[16,512,512]{1,2,0:T(8,128)(2,1)} fusion(f32[16,512,512]{1,2,0:T(8,128)} %get-tuple-element.143, f32[16,512,512]{1,2,0:T(8,128)S(1)} %bitcast.238, f32[16,512]{1,0:T(8,128)} %get-tuple-element.142, f32[16,512]{1,0:T(8,128)} %copy-done.51), kind=kLoop, calls=%fused_computation | loop fusion | flops 16777216 | bytes 42008576 | tf_op jit(solution)/shard_map/while/body/eval_jaxpr/convert_element_type | solution.py:321
  314.7 6.2 %multiply_convert_fusion.2 = bf16[16,64,512]{2,1,0:T(8,128)(2,1)S(1)} fusion(bf16[512,16,64]{0,2,1:T(8,128)(2,1)S(1)} %bitcast.252, bf16[16,512,512]{1,2,0:T(8,128)(2,1)} %multiply_convert_fusion), kind=kOutput, calls=%fused_computation.39 | convolution fusion | flops 537919488 | bytes 10485760 | tf_op jit(solution)/shard_map/while/body/eval_jaxpr/hqk,qhe->khe/dot_general | solution.py:395
  326.6 2.9 add_add_fusion.2
  359.0 123.5 %sum_grads.1 = (f32[12,32,1024]{2,1,0:T(8,128)}, f32[16,128]{1,0:T(8,128)}) custom-call(bf16[12,4,2,2,2,32,1024]{6,5,4,3,2,1,0:T(8,128)(2,1)} %constant_dynamic-update-slice_fusion.grads_ref, bf16[4,2,2,2,16,128]{5,4,3,2,1,0:T(8,128)(2,1)} %pad_maximum_fusion.2.vgrad_ref), custom_call_target="tpu_custom_call" | custom-call | tf_op jit(solution)/shard_map/sum_grads/pallas_call | solution.py:295
  (229 shorter events, 101.1 us)
Async XLA Ops:
  0.7 7.1 %copy-start.55 = (f32[32,1024]{1,0:T(8,128)S(1)}, f32[32,1024]{1,0:T(8,128)}, u32[]{:S(2)}) copy-start(f32[32,1024]{1,0:T(8,128)} %param.24) | copy-start | bytes 393220
  0.7 7.1 %copy-start.54 = (f32[32,1024]{1,0:T(8,128)S(1)}, f32[32,1024]{1,0:T(8,128)}, u32[]{:S(2)}) copy-start(f32[32,1024]{1,0:T(8,128)} %param.23) | copy-start | bytes 393220
  0.7 7.1 %copy-start.53 = (f32[32,1024]{1,0:T(8,128)S(1)}, f32[32,1024]{1,0:T(8,128)}, u32[]{:S(2)}) copy-start(f32[32,1024]{1,0:T(8,128)} %param.22) | copy-start | bytes 393220
  131.7 17.0 %copy-start.56 = (bf16[4,2,2,2,16,128]{5,4,3,2,1,0:T(8,128)(2,1)S(1)}, bf16[4,2,2,2,16,128]{5,4,3,2,1,0:T(8,128)(2,1)}, u32[]{:S(2)}) copy-start(bf16[4,2,2,2,16,128]{5,4,3,2,1,0:T(8,128)(2,1)} %get-tuple-element.73) | copy-start | bytes 393220
  131.7 17.1 %copy-start.46 = (bf16[512,1024]{1,0:T(8,128)(2,1)S(1)}, bf16[512,1024]{1,0:T(8,128)(2,1)}, u32[]{:S(2)}) copy-start(bf16[512,1024]{1,0:T(8,128)(2,1)} %param.18) | copy-start | bytes 3145732
  153.3 17.7 %copy-start.43 = (bf16[1024,512]{1,0:T(8,128)(2,1)}, bf16[1024,512]{1,0:T(8,128)(2,1)S(1)}, u32[]{:S(2)}) copy-start(bf16[1024,512]{1,0:T(8,128)(2,1)S(1)} %add_convert_fusion.4) | copy-start | bytes 3145732
  155.2 7.5 %copy-start.7 = (bf16[1024,512]{1,0:T(8,128)(2,1)}, bf16[1024,512]{1,0:T(8,128)(2,1)S(1)}, u32[]{:S(2)}) copy-start(bf16[1024,512]{1,0:T(8,128)(2,1)S(1)} %convolution_convert_fusion.13) | copy-start | bytes 3145732
  171.0 89.0 %copy-start.51 = (f32[16,512]{1,0:T(8,128)}, f32[16,512]{1,0:T(8,128)S(1)}, u32[]{:S(2)}) copy-start(f32[16,512]{1,0:T(8,128)S(1)} %log_add_fusion) | copy-start | bytes 98308
  171.0 7.9 %copy-start.4 = (bf16[1,4,2,2,2,32,1024]{6,5,4,3,2,1,0:T(8,128)(2,1)S(1)}, bf16[1,4,2,2,2,32,1024]{6,5,4,3,2,1,0:T(8,128)(2,1)}, u32[]{:S(2)}) copy-start(bf16[1,4,2,2,2,32,1024]{6,5,4,3,2,1,0:T(8,128)(2,1)} %get-tuple-element.102) | copy-start | bytes 6291460
  181.1 33.5 %copy-start.15 = (bf16[512,1024]{1,0:T(8,128)(2,1)}, bf16[512,1024]{1,0:T(8,128)(2,1)S(1)}, u32[]{:S(2)}) copy-start(bf16[512,1024]{1,0:T(8,128)(2,1)S(1)} %add_convert_fusion.2) | copy-start | bytes 3145732
  187.5 18.6 %copy-start.31 = (bf16[1,4,2,2,2,32,1024]{6,5,4,3,2,1,0:T(8,128)(2,1)S(1)}, bf16[1,4,2,2,2,32,1024]{6,5,4,3,2,1,0:T(8,128)(2,1)}, u32[]{:S(2)}) copy-start(bf16[1,4,2,2,2,32,1024]{6,5,4,3,2,1,0:T(8,128)(2,1)} %get-tuple-element.95) | copy-start | bytes 6291460
  206.1 8.5 %copy-start.9 = (bf16[512,4096]{1,0:T(8,128)(2,1)}, bf16[512,4096]{1,0:T(8,128)(2,1)S(1)}, u32[]{:S(2)}) copy-start(bf16[512,4096]{1,0:T(8,128)(2,1)S(1)} %get-tuple-element.92) | copy-start | bytes 12582916
  224.1 7.8 %copy-start.44 = (bf16[512,1024]{1,0:T(8,128)(2,1)}, bf16[512,1024]{1,0:T(8,128)(2,1)S(1)}, u32[]{:S(2)}) copy-start(bf16[512,1024]{1,0:T(8,128)(2,1)S(1)} %get-tuple-element.83) | copy-start | bytes 3145732
  242.4 3.4 copy-start.11
  242.4 3.8 copy-start.26
  260.0 9.5 %copy-start.47 = (bf16[512,1024]{1,0:T(8,128)(2,1)S(1)}, bf16[512,1024]{1,0:T(8,128)(2,1)}, u32[]{:S(2)}) copy-start(bf16[512,1024]{1,0:T(8,128)(2,1)} %param.18) | copy-start | bytes 3145732
  268.7 3.4 copy-start.18
  286.2 8.1 %slice-start = ((s8[16777216]{0:T(1024)(128)(4,1)}), s8[4194304]{0:T(1024)(128)(4,1)S(1)}, s32[]{:S(2)}) async-start(s8[16777216]{0:T(1024)(128)(4,1)} %bitcast.237), calls=%async_computation | async-start | bytes 8388608
  286.2 8.1 %slice-start.1 = ((s8[16777216]{0:T(1024)(128)(4,1)}), s8[4194304]{0:T(1024)(128)(4,1)S(1)}, s32[]{:S(2)}) async-start(s8[16777216]{0:T(1024)(128)(4,1)} %bitcast.237), calls=%async_computation.1 | async-start | bytes 8388608
  288.9 5.4 %slice-start.2 = ((s8[16777216]{0:T(1024)(128)(4,1)}), s8[4194304]{0:T(1024)(128)(4,1)S(1)}, s32[]{:S(2)}) async-start(s8[16777216]{0:T(1024)(128)(4,1)} %bitcast.237), calls=%async_computation.2 | async-start | bytes 8388608
  304.1 10.6 %copy-start.14 = (bf16[1024,512]{1,0:T(8,128)(2,1)S(1)}, bf16[1024,512]{1,0:T(8,128)(2,1)}, u32[]{:S(2)}) copy-start(bf16[1024,512]{1,0:T(8,128)(2,1)} %copy-done.13) | copy-start | bytes 3145732
  314.7 6.2 %copy-start = (bf16[16,512,512]{1,2,0:T(8,128)(2,1)S(1)}, bf16[16,512,512]{1,2,0:T(8,128)(2,1)}, u32[]{:S(2)}) copy-start(bf16[16,512,512]{1,2,0:T(8,128)(2,1)} %multiply_convert_fusion) | copy-start | bytes 25165828
  314.7 6.2 %copy-start.8 = (bf16[1024,512]{1,0:T(8,128)(2,1)S(1)}, bf16[1024,512]{1,0:T(8,128)(2,1)}, u32[]{:S(2)}) copy-start(bf16[1024,512]{1,0:T(8,128)(2,1)} %copy-done.7) | copy-start | bytes 3145732
  326.6 3.8 copy-start.48
  (43 other events, 102.7 us)

commit v2 on v0

--- a/solution.py
+++ b/solution.py
@@ -1,7 +1,127 @@
+import functools
+
 import jax
 import jax.numpy as jnp
 from jax import lax
+from jax.experimental import pallas as pl
+from jax.experimental.pallas import tpu as pltpu
 from jax.sharding import PartitionSpec as P
+
+MESH = pl.DeviceIdType.MESH
+BLOCKS = 12
+
+
+def place():
+    dp = lax.axis_index("dp")
+    fs = lax.axis_index("fsdp")
+    return dp // 2, dp % 2, fs // 2, fs % 2
+
+
+def device(z, x, y, c):
+    return (z * 2 + x, y * 2 + c)
+
+
+def greet(depth):
+    z, x, y, c = place()
+    peers = [device(z, x, y, 1 - c), device(z, 1 - x, y, c), device(z, x, 1 - y, c)]
+    peers += [device((z + k) % depth, x, y, c) for k in range(1, depth)]
+    bar = pltpu.get_barrier_semaphore()
+    for peer in peers:
+        pl.semaphore_signal(bar, inc=1, device_id=peer, device_id_type=MESH)
+    pl.semaphore_wait(bar, len(peers))
+
+
+def send(src, dst, ssem, rsem, peer):
+    return pltpu.make_async_remote_copy(
+        src_ref=src, dst_ref=dst, send_sem=ssem, recv_sem=rsem, device_id=peer, device_id_type=MESH
+    )
+
+
+class GatherBlock:
+    def __init__(self, full, mine, ss, rs, depth):
+        self.full, self.ss, self.rs, self.depth = full, ss, rs, depth
+        self.mine = mine
+        z, x, y, c = self.at = place()
+        self.xn, self.yn, self.cn = device(z, 1 - x, y, c), device(z, x, 1 - y, c), device(z, x, y, 1 - c)
+        half = depth // 2
+        self.low, self.high = pl.ds(0, half), pl.ds(half, depth - half)
+
+    def moves(self):
+        z, x, y, c = self.at
+        full, ss, rs = self.full, self.ss, self.rs
+        every = pl.ds(0, self.depth)
+        out = {}
+        own = full.at[z, x, y, c]
+        for k in range(1, self.depth):
+            out["col", k] = send(own, own, ss.at[k - 1], rs.at[k - 1], device((z + k) % self.depth, x, y, c))
+        base = self.depth - 1
+        column = full.at[every, x, y, c]
+        out["x"] = send(column, column, ss.at[base], rs.at[base], self.xn)
+        out["y"] = send(column, column, ss.at[base + 1], rs.at[base + 1], self.yn)
+        out["c0"] = send(column, column, ss.at[base + 2], rs.at[base + 2], self.cn)
+        xcol = full.at[every, 1 - x, y, c]
+        ycol = full.at[every, x, 1 - y, c]
+        out["c1"] = send(xcol, xcol, ss.at[base + 3], rs.at[base + 3], self.cn)
+        out["c2"] = send(ycol, ycol, ss.at[base + 4], rs.at[base + 4], self.cn)
+        xlow = full.at[self.low, 1 - x, y, c]
+        yhigh = full.at[self.high, x, 1 - y, c]
+        out["dy"] = send(xlow, xlow, ss.at[base + 5], rs.at[base + 5], self.yn)
+        out["dx"] = send(yhigh, yhigh, ss.at[base + 6], rs.at[base + 6], self.xn)
+        dcol = full.at[every, 1 - x, 1 - y, c]
+        out["c3"] = send(dcol, dcol, ss.at[base + 7], rs.at[base + 7], self.cn)
+        return out
+
+    def arrivals(self):
+        z, x, y, c = self.at
+        full, ss, rs = self.full, self.ss, self.rs
+        every = pl.ds(0, self.depth)
+        out = {}
+
+        def got(ref, i):
+            return send(ref, ref, ss.at[i], rs.at[i], self.cn)
+
+        for k in range(1, self.depth):
+            out["col", k] = got(full.at[(z + self.depth - k) % self.depth, x, y, c], k - 1)
+        base = self.depth - 1
+        out["x"] = got(full.at[every, 1 - x, y, c], base)
+        out["y"] = got(full.at[every, x, 1 - y, c], base + 1)
+        out["c0"] = got(full.at[every, x, y, 1 - c], base + 2)
+        out["c1"] = got(full.at[every, 1 - x, y, 1 - c], base + 3)
+        out["c2"] = got(full.at[every, x, 1 - y, 1 - c], base + 4)
+        out["dy"] = got(full.at[self.low, 1 - x, 1 - y, c], base + 5)
+        out["dx"] = got(full.at[self.high, 1 - x, 1 - y, c], base + 6)
+        out["c3"] = got(full.at[every, 1 - x, 1 - y, 1 - c], base + 7)
+        return out
+
+    def stage(self, s):
+        moves, arrivals = self.moves(), self.arrivals()
+        if s == 0:
+            z, x, y, c = self.at
+            self.full[z, x, y, c] = self.mine()
+            for k in range(1, self.depth):
+                moves["col", k].start()
+        if s == 1:
+            for k in range(1, self.depth):
+                arrivals["col", k].wait_recv()
+            for name in ("x", "y", "c0"):
+                moves[name].start()
+        if s == 2:
+            arrivals["x"].wait_recv()
+            moves["dy"].start()
+            moves["c1"].start()
+            arrivals["y"].wait_recv()
+            moves["dx"].start()
+            moves["c2"].start()
+        if s == 3:
+            arrivals["dy"].wait_recv()
+            arrivals["dx"].wait_recv()
+            moves["c3"].start()
+        if s == 4:
+            for name in ("c0", "c1", "c2", "c3"):
+                arrivals[name].wait_recv()
+            for move in moves.values():
+                move.wait_send()
+
 
 HEAD = 64
 
@@ -98,7 +218,7 @@
     )
 
 
-def per_device(
+def plain_device(
     tokens,
     segment,
     cotangent,
@@ -369,7 +489,734 @@
     )
 
 
+ATTN = 4
+LANES = 128
+SIDE = 256
+
+
+def aligned(start, size, step=None):
+    return pl.ds(pl.multiple_of(start, step or size), size)
+
+
+def side_loop(count, body):
+    def step(i, carry):
+        body(i)
+        return carry
+
+    lax.fori_loop(0, count, step, 0)
+
+
+def square(full, b):
+    size = full.shape[-1]
+    return full.at[b].reshape(size, size)
+
+
+def spread_vectors(tiles, short_ref, up_ref, depth):
+    for dp in range(2 * depth):
+        total = jnp.zeros((16, LANES), jnp.float32)
+        for fs in range(4):
+            total = total + tiles[dp // 2, dp % 2, fs // 2, fs % 2].astype(jnp.float32)
+        short_ref[:, dp * LANES : (dp + 1) * LANES] = total[:8]
+        for fs in range(4):
+            at = (dp * 4 + fs) * LANES
+            up_ref[:, at : at + LANES] = total[8 + fs : 9 + fs]
+
+
+def project(x_ref, weight, out_ref, bias=None, scale=None):
+    def step(n):
+        cols = aligned(n * SIDE, SIDE)
+        got = matmul(x_ref[...], weight[:, cols])
+        if bias is not None:
+            got = got + bias[:, cols]
+        got = to_half(got)
+        if scale is not None:
+            got = got * scale
+        out_ref[:, cols] = got
+
+    side_loop(weight.shape[1] // SIDE, step)
+
+
+def attend_pairs(first, last, qkvc, lse, mask):
+    length = mask.shape[0]
+
+    def pair(p):
+        lanes = aligned(p * LANES, LANES)
+        q, k, v = qkvc[0, :, lanes], qkvc[1, :, lanes], qkvc[2, :, lanes]
+        lane = lax.broadcasted_iota(jnp.int32, (length, LANES), 1)
+        lower = lane < HEAD
+        total = jnp.zeros((length, LANES), jnp.float32)
+        logs = lse[...]
+        for h in range(2):
+            here = lower if h == 0 else jnp.logical_not(lower)
+            key = jnp.where(here, k, jnp.zeros_like(k))
+            scores = matmul_nt(q, key) + mask[...]
+            row_max = jnp.max(scores, axis=-1, keepdims=True)
+            row_exp = jnp.exp(scores - row_max)
+            row_total = jnp.sum(row_exp, axis=-1, keepdims=True)
+            part = matmul(to_half(row_exp), v) / row_total
+            total = jnp.where(here, part, total)
+            logs = jnp.where(lane == 2 * p + h, row_max + jnp.log(row_total), logs)
+        qkvc[3, :, lanes] = to_half(total)
+        lse[...] = logs
+
+    def step(i, carry):
+        pair(i)
+        return carry
+
+    lax.fori_loop(first, last, step, 0)
+
+
+def forward_kernel(
+    depth, tokens, segment, cotangent, wq, wk, wv, wo, up_w, down_w, short_in, up_in,
+    out_hbm, full_hbm, qkvc_hbm, lse_hbm, mid_hbm, act_hbm, dge_hbm, nhat_hbm, rstd_hbm, dsec_hbm, small_hbm,
+    full, tiles, mine_vec, short, up_bias, qkvc, lse, lse_turned, mask, mid, act, dge, nhat, rstd, total, final,
+    small, ss, rs, osem, wsem,
+):
+    length, width = tokens.shape
+    z, x, y, c = place()
+    fs = y * 2 + c
+    rows = wq.shape[0]
+    greet(depth)
+
+    mine_vec[...] = jnp.zeros_like(mine_vec)
+    mine_vec[0:8, 0:rows] = short_in[...]
+    placed = pltpu.roll(mine_vec[...], fs * rows, 1)
+    row_at = lax.broadcasted_iota(jnp.int32, (16, LANES), 0)
+    mine_vec[...] = jnp.where(row_at == 8 + fs, jnp.broadcast_to(up_in[...], (16, LANES)), placed)
+
+    def own(b):
+        if b < ATTN:
+            return to_half((wq, wk, wv, wo)[b][...])
+        if b < 2 * ATTN:
+            at = (b - ATTN) * width
+            return to_half(up_w[:, at : at + width])
+        at = (b - 2 * ATTN) * width
+        return to_half(down_w[:, at : at + width])
+
+    def block(b):
+        return GatherBlock(full.at[b], lambda: own(b), ss.at[b], rs.at[b], depth)
+
+    vec = GatherBlock(tiles, lambda: to_half(mine_vec[...]), ss.at[BLOCKS], rs.at[BLOCKS], depth)
+
+    def keep(b):
+        return pltpu.make_async_copy(full.at[b], full_hbm.at[b], wsem.at[b])
+
+    flushed = []
+
+    def flush(src, dst):
+        copy = pltpu.make_async_copy(src, dst, osem.at[len(flushed)])
+        copy.start()
+        flushed.append(copy)
+
+    def pump(t):
+        for s in range(5):
+            b = t - s
+            if 0 <= b < BLOCKS:
+                block(b).stage(s)
+                if s == 4:
+                    keep(b).start()
+            if b == 0:
+                vec.stage(s)
+
+    pump(0)
+    pump(1)
+    labels = segment[...].astype(jnp.float32)
+    turned = jnp.transpose(jnp.broadcast_to(labels, (LANES, length)))
+    mask[...] = jnp.where(turned[:, :1] == labels, 0.0, masked_score)
+    valid = jnp.where(turned[:, :1] >= 0.0, 1.0, 0.0)
+    lse[...] = jnp.zeros_like(lse)
+    pump(2)
+    pump(3)
+    pump(4)
+    spread_vectors(tiles, short, up_bias, depth)
+    project(tokens, square(full, 0), qkvc.at[0], short.at[0:1], 0.125)
+    pump(5)
+    project(tokens, square(full, 1), qkvc.at[1])
+    pump(6)
+    project(tokens, square(full, 2), qkvc.at[2], short.at[1:2])
+    attend_pairs(0, 4, qkvc, lse, mask)
+    pump(7)
+    attend_pairs(4, 8, qkvc, lse, mask)
+    flush(qkvc, qkvc_hbm)
+    lse_turned[...] = jnp.transpose(lse[...])
+    flush(lse_turned, lse_hbm)
+    pump(8)
+
+    wo_full = square(full, 3)
+
+    def attended(n):
+        cols = aligned(n * SIDE, SIDE)
+        total[:, cols] = (
+            matmul(qkvc[3], wo_full[:, cols]) + short[2:3, cols] + tokens[:, cols].astype(jnp.float32)
+        )
+
+    side_loop(width // SIDE, attended)
+
+    def first_norm(i):
+        at = aligned(i * LANES, LANES)
+        values = total[at, :]
+        center = values - jnp.mean(values, axis=-1, keepdims=True)
+        spread = jnp.mean(center * center, axis=-1, keepdims=True)
+        r = lax.rsqrt(spread + norm_epsilon)
+        unit = center * r
+        nhat[at, :] = unit
+        rstd[at, :] = jnp.broadcast_to(r, (LANES, LANES))
+        mid[at, :] = to_half(unit * short[4:5, :] + short[5:6, :])
+
+    side_loop(length // LANES, first_norm)
+    flush(nhat, nhat_hbm)
+    flush(rstd, rstd_hbm)
+    flush(mid, mid_hbm)
+
+    def activate(j):
+        weight = square(full, ATTN + j)
+
+        def step(n):
+            cols = aligned(n * SIDE, SIDE)
+            pre = matmul(mid[...], weight[:, cols]) + up_bias[:, aligned(j * width + n * SIDE, SIDE)]
+            cdf = 0.5 * (1.0 + lax.erf(pre * 0.7071067811865476))
+            act[j, :, cols] = to_half(pre * cdf)
+            pdf = jnp.exp(-0.5 * pre * pre) * 0.3989422804014327
+            dge[j, :, cols] = to_half(cdf + pre * pdf)
+
+        side_loop(width // SIDE, step)
+        flush(act.at[j], act_hbm.at[j])
+        flush(dge.at[j], dge_hbm.at[j])
+
+    def contract(j):
+        weight = square(full, 2 * ATTN + j)
+
+        def step(n):
+            cols = aligned(n * SIDE, SIDE)
+            got = matmul_nt(act[j], weight[cols, :])
+            if j == 0:
+                total[:, cols] = got + short[3:4, cols] + mid[:, cols].astype(jnp.float32)
+            else:
+                total[:, cols] = total[:, cols] + got
+
+        side_loop(width // SIDE, step)
+
+    for j in range(ATTN):
+        activate(j)
+        pump(9 + j)
+    for j in range(ATTN):
+        contract(j)
+        if j < ATTN - 1:
+            pump(13 + j)
+
+    small[...] = jnp.zeros_like(small)
+    small[0:1, :] = short[4:5, :]
+
+    def second_norm(i):
+        at = aligned(i * LANES, LANES)
+        values = total[at, :]
+        center = values - jnp.mean(values, axis=-1, keepdims=True)
+        spread = jnp.mean(center * center, axis=-1, keepdims=True)
+        r = lax.rsqrt(spread + norm_epsilon)
+        unit = center * r
+        gain = short[6:7, :]
+        final[at, :] = to_half(unit * gain + short[7:8, :])
+        e = cotangent[at, :].astype(jnp.float32) * lse[at, 0:1]
+        small[1:2, :] = small[1:2, :] + jnp.sum(e * unit, axis=0, keepdims=True)
+        small[2:3, :] = small[2:3, :] + jnp.sum(e, axis=0, keepdims=True)
+        eg = e * gain
+        d = r * (
+            eg - jnp.mean(eg, axis=-1, keepdims=True) - unit * jnp.mean(eg * unit, axis=-1, keepdims=True)
+        )
+        total[at, :] = d
+        small[3:4, :] = small[3:4, :] + jnp.sum(to_half(d).astype(jnp.float32), axis=0, keepdims=True)
+
+    lse[...] = jnp.broadcast_to(valid, lse.shape)
+    side_loop(length // LANES, second_norm)
+    flush(final, out_hbm)
+    flush(total, dsec_hbm)
+    flush(small, small_hbm)
+    for copy in flushed:
+        copy.wait()
+    for b in range(BLOCKS):
+        keep(b).wait()
+
+
+def forward_call(depth, tokens, segment, cotangent, wq, wk, wv, wo, up_w, down_turned, short, up_bias):
+    length, width = tokens.shape
+    rows = wq.shape[0]
+    dims = (depth, 2, 2, 2)
+    bf, f32 = jnp.bfloat16, jnp.float32
+    shapes = [
+        ((length, width), bf),
+        ((BLOCKS,) + dims + (rows, width), bf),
+        ((4, length, width), bf),
+        ((LANES, length), f32),
+        ((length, width), bf),
+        ((ATTN, length, width), bf),
+        ((ATTN, length, width), bf),
+        ((length, width), f32),
+        ((length, LANES), f32),
+        ((length, width), f32),
+        ((8, width), f32),
+    ]
+    n = depth + 7
+    scratch = [
+        pltpu.VMEM((BLOCKS,) + dims + (rows, width), bf),
+        pltpu.VMEM(dims + (16, LANES), bf),
+        pltpu.VMEM((16, LANES), f32),
+        pltpu.VMEM((8, width), f32),
+        pltpu.VMEM((1, ATTN * width), f32),
+        pltpu.VMEM((4, length, width), bf),
+        pltpu.VMEM((length, LANES), f32),
+        pltpu.VMEM((LANES, length), f32),
+        pltpu.VMEM((length, length), f32),
+        pltpu.VMEM((length, width), bf),
+        pltpu.VMEM((ATTN, length, width), bf),
+        pltpu.VMEM((ATTN, length, width), bf),
+        pltpu.VMEM((length, width), f32),
+        pltpu.VMEM((length, LANES), f32),
+        pltpu.VMEM((length, width), f32),
+        pltpu.VMEM((length, width), bf),
+        pltpu.VMEM((8, width), f32),
+        pltpu.SemaphoreType.DMA((BLOCKS + 1, n)),
+        pltpu.SemaphoreType.DMA((BLOCKS + 1, n)),
+        pltpu.SemaphoreType.DMA((16,)),
+        pltpu.SemaphoreType.DMA((BLOCKS,)),
+    ]
+    return pl.pallas_call(
+        functools.partial(forward_kernel, depth),
+        out_shape=tuple(jax.ShapeDtypeStruct(*s) for s in shapes),
+        in_specs=[pl.BlockSpec(memory_space=pltpu.VMEM)] * 11,
+        out_specs=tuple(pl.BlockSpec(memory_space=pl.ANY) for _ in shapes),
+        scratch_shapes=scratch,
+        compiler_params=pltpu.CompilerParams(
+            collective_id=0, has_side_effects=True, vmem_limit_bytes=60 * 2**20
+        ),
+        name="forward",
+    )(tokens, segment, cotangent, wq, wk, wv, wo, up_w, down_turned, short, up_bias)
+
+
+class SumBlock:
+    def __init__(self, grad, held, r0, r1x, r1y, r2x, r2y, r3, ss, rs, depth):
+        self.grad, self.held = grad, held
+        self.r0, self.r1x, self.r1y, self.r2x, self.r2y, self.r3 = r0, r1x, r1y, r2x, r2y, r3
+        self.ss, self.rs, self.depth = ss, rs, depth
+        self.at = place()
+
+    def move(self, name, k=0):
+        z, x, y, c = self.at
+        xn, yn = device(z, 1 - x, y, c), device(z, x, 1 - y, c)
+        g, h, ss, rs, depth = self.grad, self.held, self.ss, self.rs, self.depth
+        half = depth // 2
+        low, high, every, both = pl.ds(0, half), pl.ds(half, depth - half), pl.ds(0, depth), pl.ds(0, 2)
+        if name == "c":
+            return send(g.at[every, both, both, 1 - c], self.r0, ss.at[0], rs.at[0], device(z, x, y, 1 - c))
+        if name == "dx":
+            return send(h.at[low, 1 - x, 1 - y], self.r1x, ss.at[1], rs.at[1], xn)
+        if name == "dy":
+            return send(h.at[high, 1 - x, 1 - y], self.r1y, ss.at[2], rs.at[2], yn)
+        if name == "x":
+            return send(h.at[every, 1 - x, y], self.r2x, ss.at[3], rs.at[3], xn)
+        if name == "y":
+            return send(h.at[every, x, 1 - y], self.r2y, ss.at[4], rs.at[4], yn)
+        there = (z + k) % depth
+        return send(h.at[there, x, y], self.r3.at[k - 1], ss.at[4 + k], rs.at[4 + k], device(there, x, y, c))
+
+    def stage(self, s, out=None):
+        z, x, y, c = self.at
+        g, h, depth = self.grad, self.held, self.depth
+        half = depth // 2
+        if s == 0:
+            self.move("c").start()
+        if s == 1:
+            self.move("c").wait()
+            for zz in range(depth):
+                h[zz, 1 - x, 1 - y] = g[zz, 1 - x, 1 - y, c] + self.r0[zz, 1 - x, 1 - y]
+            self.move("dx").start()
+            self.move("dy").start()
+            for xx, yy in ((1 - x, y), (x, 1 - y), (x, y)):
+                for zz in range(depth):
+                    h[zz, xx, yy] = g[zz, xx, yy, c] + self.r0[zz, xx, yy]
+        if s == 2:
+            self.move("dx").wait_recv()
+            self.move("dy").wait_recv()
+            for zz in range(half):
+                h[zz, x, 1 - y] = h[zz, x, 1 - y] + self.r1x[zz]
+            self.move("y").start()
+            for zz in range(half, depth):
+                h[zz, 1 - x, y] = h[zz, 1 - x, y] + self.r1y[zz - half]
+            self.move("x").start()
+        if s == 3:
+            self.move("x").wait_recv()
+            self.move("y").wait_recv()
+            for k in list(range(1, depth)) + [0]:
+                zz = (z + k) % depth
+                total = (
+                    h[zz, x, y].astype(jnp.float32)
+                    + self.r2x[zz].astype(jnp.float32)
+                    + self.r2y[zz].astype(jnp.float32)
+                )
+                h[zz, x, y] = total.astype(jnp.bfloat16)
+                if k:
+                    self.move("z", k).start()
+        if s == 4:
+            total = h[z, x, y].astype(jnp.float32)
+            for k in range(1, depth):
+                self.move("z", k).wait_recv()
+                total = total + self.r3[k - 1].astype(jnp.float32)
+            out[...] = total
+            for name in ("dx", "dy", "x", "y"):
+                self.move(name).wait_send()
+            for k in range(1, depth):
+                self.move("z", k).wait_send()
+
+
+SLOTS = (2, 4, 2, 4, 4, 4, 4, 4)
+
+
+def sum_scratch(depth, rows, cols, slots, blocks):
+    bf = jnp.bfloat16
+    half = depth // 2
+    shapes = [
+        (depth, 2, 2, 2), (depth, 2, 2), (depth, 2, 2), (half,), (depth - half,), (depth,), (depth,), (depth - 1,),
+    ]
+    return [pltpu.VMEM((n,) + s + (rows, cols), bf) for n, s in zip(slots, shapes)] + [
+        pltpu.SemaphoreType.DMA((blocks, depth + 4)),
+        pltpu.SemaphoreType.DMA((blocks, depth + 4)),
+    ]
+
+
+def attend_back_pairs(first, last, qkvc, lse, delta, mask, grads):
+    length = mask.shape[0]
+
+    def pair(p, carry):
+        lanes = aligned(p * LANES, LANES)
+        q, k, v, d_context = qkvc[0, :, lanes], qkvc[1, :, lanes], qkvc[2, :, lanes], grads[3, :, lanes]
+        lower = lax.broadcasted_iota(jnp.int32, (length, LANES), 1) < HEAD
+        sums = [jnp.zeros((length, LANES), jnp.float32) for _ in range(3)]
+        for h in range(2):
+            here = lower if h == 0 else jnp.logical_not(lower)
+            row = pl.ds(2 * p + h, 1)
+            key = jnp.where(here, k, jnp.zeros_like(k))
+            value = jnp.where(here, v, jnp.zeros_like(v))
+            probs = jnp.exp(matmul_nt(key, q) + mask[...] - lse[row, :])
+            d_scores = to_half(probs * (matmul_nt(value, d_context) - delta[row, :]))
+            parts = (
+                contract_rows(d_scores, k) * 0.125,
+                matmul(d_scores, q),
+                matmul(to_half(probs), d_context),
+            )
+            sums = [jnp.where(here, part, total) for part, total in zip(parts, sums)]
+        for i in range(3):
+            grads[i, :, lanes] = to_half(sums[i])
+        return carry
+
+    lax.fori_loop(first, last, pair, 0)
+
+
+WEIGHT_SLOTS = 6
+WEIGHT_ORDER = (8, 4, 9, 5, 10, 6, 11, 7, 3, 2, 1, 0)
+
+
+def backward_kernel(
+    depth, tokens_hbm, segment, full_hbm, qkvc_hbm, lse_hbm, mid_hbm, act_hbm, dge_hbm, nhat_hbm, rstd_hbm,
+    dsec_hbm, small,
+    dtok_hbm, gq, gk, gv, go, gup, gdown, gshort, gup_bias,
+    tokens, qkvc, lse, mid, act, dge, nhat, rstd, total, half, turn_a, turn_b, mask, delta, delta_turned, weights,
+    short, up_bias, tile_sum, *rest,
+):
+    big, vec, (isem, wsem, osem) = rest[:10], rest[10:20], rest[20:]
+    length, width = tokens.shape
+    rows = gq.shape[0]
+    z, x, y, c = place()
+    fs = y * 2 + c
+    f32 = jnp.float32
+
+    loads = {}
+    for name, src, dst in (
+        ("dsec", dsec_hbm, total),
+        ("act0", act_hbm.at[0], act.at[0]),
+        ("w0", None, None),
+        ("dge0", dge_hbm.at[0], dge.at[0]),
+        ("w1", None, None),
+        ("act1", act_hbm.at[1], act.at[1]),
+        ("w2", None, None),
+        ("dge1", dge_hbm.at[1], dge.at[1]),
+        ("w3", None, None),
+        ("act2", act_hbm.at[2], act.at[2]),
+        ("w4", None, None),
+        ("dge2", dge_hbm.at[2], dge.at[2]),
+        ("w5", None, None),
+        ("act3", act_hbm.at[3], act.at[3]),
+        ("dge3", dge_hbm.at[3], dge.at[3]),
+        ("mid", mid_hbm, mid),
+        ("nhat", nhat_hbm, nhat),
+        ("rstd", rstd_hbm, rstd),
+        ("qkvc", qkvc_hbm, qkvc),
+        ("lse", lse_hbm, lse),
+        ("tokens", tokens_hbm, tokens),
+    ):
+        if src is None:
+            i = int(name[1:])
+            loads[name] = pltpu.make_async_copy(full_hbm.at[WEIGHT_ORDER[i]], weights.at[i], wsem.at[i])
+        else:
+            loads[name] = pltpu.make_async_copy(src, dst, isem.at[len(loads)])
+        loads[name].start()
+
+    def weight(i):
+        loads["w%d" % i].wait()
+        return square(weights, i % WEIGHT_SLOTS)
+
+    def refill(i):
+        n = i + WEIGHT_SLOTS
+        if n < BLOCKS:
+            loads["w%d" % n] = pltpu.make_async_copy(
+                full_hbm.at[WEIGHT_ORDER[n]], weights.at[i % WEIGHT_SLOTS], wsem.at[n]
+            )
+            loads["w%d" % n].start()
+
+    greet(depth)
+
+    outs = [gdown.at[:, i * width : (i + 1) * width] for i in range(4)]
+    outs += [gup.at[:, i * width : (i + 1) * width] for i in range(4)] + [go, gv, gk, gq]
+
+    def block(b):
+        return SumBlock(
+            *[ref.at[b % n] for ref, n in zip(big[:8], SLOTS)], big[8].at[b], big[9].at[b], depth
+        )
+
+    vblock = SumBlock(*[ref.at[0] for ref in vec[:8]], vec[8].at[0], vec[9].at[0], depth)
+
+    def pump(t):
+        for s in (1, 0, 2, 3, 4):
+            b = t - s
+            if 0 <= b < BLOCKS:
+                block(b).stage(s, outs[b])
+            if b == BLOCKS - 1:
+                vblock.stage(s, tile_sum)
+
+    def weight_grad(b, left, right):
+        part = width // depth
+
+        def step(zz):
+            got = to_half(matmul(left[aligned(zz * part, part), :], right[...]))
+            big[0][b % SLOTS[0], zz] = got.reshape(2, 2, 2, rows, width)
+
+        side_loop(depth, step)
+
+    def sums_of(ref, cols):
+        return jnp.sum(ref.astype(f32), axis=0, keepdims=True)
+
+    loads["dsec"].wait()
+    half[...] = to_half(total[...])
+    turn_a[...] = jnp.transpose(half[...])
+    loads["act0"].wait()
+    weight_grad(0, turn_a, act.at[0])
+    pump(0)
+
+    labels = segment[...].astype(f32)
+    turned = jnp.transpose(jnp.broadcast_to(labels, (LANES, length)))
+    mask[...] = jnp.where(turned[:, :1] == labels, 0.0, masked_score)
+    short[...] = jnp.zeros_like(short)
+    short[3:4, :] = small[3:4, :]
+    short[6:7, :] = small[1:2, :]
+    short[7:8, :] = small[2:3, :]
+
+    def into_units(j):
+        w = weight(2 * j)
+        loads["dge%d" % j].wait()
+
+        def step(n):
+            cols = aligned(n * SIDE, SIDE)
+            d_pre = to_half(matmul(half[...], w[:, cols]) * dge[j, :, cols].astype(f32))
+            dge[j, :, cols] = d_pre
+            up_bias[:, aligned(j * width + n * SIDE, SIDE)] = sums_of(d_pre, cols)
+
+        side_loop(width // SIDE, step)
+        refill(2 * j)
+
+    def add_product(left, w, cols):
+        total[:, cols] = total[:, cols] + matmul_nt(left[...], w[cols, :])
+
+    def out_of_units(j):
+        w = weight(2 * j + 1)
+
+        side_loop(width // SIDE, lambda n: add_product(dge.at[j], w, aligned(n * SIDE, SIDE)))
+        refill(2 * j + 1)
+
+    for j in range(4):
+        into_units(j)
+        out_of_units(j)
+        if j < 3:
+            loads["act%d" % (j + 1)].wait()
+            weight_grad(j + 1, turn_a, act.at[j + 1])
+            pump(j + 1)
+
+    loads["mid"].wait()
+    turn_b[...] = jnp.transpose(mid[...])
+    weight_grad(4, turn_b, dge.at[0])
+    pump(4)
+
+    loads["nhat"].wait()
+    loads["rstd"].wait()
+
+    def first_norm(i):
+        at = aligned(i * LANES, LANES)
+        e = total[at, :]
+        unit = nhat[at, :]
+        short[4:5, :] = short[4:5, :] + jnp.sum(e * unit, axis=0, keepdims=True)
+        short[5:6, :] = short[5:6, :] + jnp.sum(e, axis=0, keepdims=True)
+        eg = e * small[0:1, :]
+        d = rstd[at, 0:1] * (
+            eg - jnp.mean(eg, axis=-1, keepdims=True) - unit * jnp.mean(eg * unit, axis=-1, keepdims=True)
+        )
+        total[at, :] = d
+        d_half = to_half(d)
+        half[at, :] = d_half
+        short[2:3, :] = short[2:3, :] + jnp.sum(d_half.astype(f32), axis=0, keepdims=True)
+
+    side_loop(length // LANES, first_norm)
+    loads["qkvc"].wait()
+    loads["lse"].wait()
+    wo = weight(8)
+    delta[...] = jnp.zeros_like(delta)
+
+    def context_back(n):
+        cols = aligned(n * SIDE, SIDE)
+        d_context = to_half(matmul_nt(half[...], wo[cols, :]))
+        act[3, :, cols] = d_context
+        product = d_context.astype(f32) * qkvc[3, :, cols].astype(f32)
+        lane = lax.broadcasted_iota(jnp.int32, (length, LANES), 1)
+        got = delta[...]
+        for i in range(SIDE // HEAD):
+            two = product[:, (i // 2) * LANES : (i // 2 + 1) * LANES]
+            here = lane // HEAD == i % 2
+            head = jnp.sum(jnp.where(here, two, 0.0), axis=-1, keepdims=True)
+            got = jnp.where(lane == n * (SIDE // HEAD) + i, head, got)
+        delta[...] = got
+
+    side_loop(width // SIDE, context_back)
+    delta_turned[...] = jnp.transpose(delta[...])
+    weight_grad(5, turn_b, dge.at[1])
+    pump(5)
+    attend_back_pairs(0, 3, qkvc, lse, delta_turned, mask, act)
+    weight_grad(6, turn_b, dge.at[2])
+    pump(6)
+    attend_back_pairs(3, 6, qkvc, lse, delta_turned, mask, act)
+    weight_grad(7, turn_b, dge.at[3])
+    pump(7)
+    attend_back_pairs(6, 8, qkvc, lse, delta_turned, mask, act)
+    turn_a[...] = jnp.transpose(qkvc[3])
+    weight_grad(8, turn_a, half)
+    pump(8)
+    loads["tokens"].wait()
+    turn_b[...] = jnp.transpose(tokens[...])
+    weight_grad(9, turn_b, act.at[2])
+    pump(9)
+    weight_grad(10, turn_b, act.at[1])
+    pump(10)
+
+    def bias_sums(n):
+        cols = aligned(n * SIDE, SIDE)
+        short[0:1, cols] = sums_of(act[0, :, cols], cols)
+        short[1:2, cols] = sums_of(act[2, :, cols], cols)
+
+    side_loop(width // SIDE, bias_sums)
+    for dp in range(2 * depth):
+        for fsdp in range(4):
+            at = (dp * 4 + fsdp) * LANES
+            vec[0][0, dp // 2, dp % 2, fsdp // 2, fsdp % 2] = to_half(
+                jnp.concatenate(
+                    [
+                        short[:, dp * LANES : (dp + 1) * LANES],
+                        jnp.broadcast_to(up_bias[:, at : at + LANES], (8, LANES)),
+                    ],
+                    axis=0,
+                )
+            )
+    weight_grad(11, turn_b, act.at[0])
+    pump(11)
+    for i, (w, j) in enumerate(((9, 2), (10, 1), (11, 0))):
+        w = weight(w)
+        side_loop(width // SIDE, lambda n: add_product(act.at[j], w, aligned(n * SIDE, SIDE)))
+        if i == 2:
+            done = pltpu.make_async_copy(total, dtok_hbm, osem.at[0])
+            done.start()
+        pump(12 + i)
+    pump(15)
+    moved = pltpu.roll(tile_sum[...], (4 - fs) * rows % LANES, 1)
+    gshort[...] = moved[:8]
+    gup_bias[...] = tile_sum[8:9, :]
+    done.wait()
+
+
+def backward_call(depth, tokens, segment, full, qkvc, lse, mid, act, dge, nhat, rstd, dsec, small):
+    length, width = tokens.shape
+    rows = full.shape[-2]
+    bf, f32 = jnp.bfloat16, jnp.float32
+    part = ((rows, width), f32)
+    shapes = [
+        ((length, width), f32), part, part, part, part, ((rows, 4 * width), f32), ((rows, 4 * width), f32),
+        ((8, LANES), f32), ((1, LANES), f32),
+    ]
+    vmem, hbm = pl.BlockSpec(memory_space=pltpu.VMEM), pl.BlockSpec(memory_space=pl.ANY)
+    scratch = [
+        pltpu.VMEM((length, width), bf),
+        pltpu.VMEM((4, length, width), bf),
+        pltpu.VMEM((LANES, length), f32),
+        pltpu.VMEM((length, width), bf),
+        pltpu.VMEM((4, length, width), bf),
+        pltpu.VMEM((4, length, width), bf),
+        pltpu.VMEM((length, width), f32),
+        pltpu.VMEM((length, LANES), f32),
+        pltpu.VMEM((length, width), f32),
+        pltpu.VMEM((length, width), bf),
+        pltpu.VMEM((width, length), bf),
+        pltpu.VMEM((width, length), bf),
+        pltpu.VMEM((length, length), f32),
+        pltpu.VMEM((length, LANES), f32),
+        pltpu.VMEM((LANES, length), f32),
+        pltpu.VMEM((WEIGHT_SLOTS,) + full.shape[1:], bf),
+        pltpu.VMEM((8, width), f32),
+        pltpu.VMEM((1, 4 * width), f32),
+        pltpu.VMEM((16, LANES), f32),
+    ]
+    scratch += sum_scratch(depth, rows, width, SLOTS, BLOCKS)
+    scratch += sum_scratch(depth, 16, LANES, (1,) * 8, 1)
+    scratch += [pltpu.SemaphoreType.DMA((24,)), pltpu.SemaphoreType.DMA((BLOCKS,)), pltpu.SemaphoreType.DMA((1,))]
+    return pl.pallas_call(
+        functools.partial(backward_kernel, depth),
+        out_shape=tuple(jax.ShapeDtypeStruct(*s) for s in shapes),
+        in_specs=[hbm, vmem] + [hbm] * 9 + [vmem],
+        out_specs=tuple([hbm] + [vmem] * 8),
+        scratch_shapes=scratch,
+        compiler_params=pltpu.CompilerParams(
+            collective_id=1, has_side_effects=True, vmem_limit_bytes=60 * 2**20
+        ),
+        name="backward",
+    )(tokens, segment, full, qkvc, lse, mid, act, dge, nhat, rstd, dsec, small)
+
+
+def kernel_device(
+    tokens, segment, cotangent, query_w, key_w, value_w, attn_out_w, up_w, down_w, query_bias, value_bias,
+    attn_out_bias, up_bias, down_bias, norm1_gain, norm1_shift, norm2_gain, norm2_shift,
+):
+    depth = lax.axis_size("dp") // 2
+    short = jnp.stack(
+        [query_bias, value_bias, attn_out_bias, down_bias, norm1_gain, norm1_shift, norm2_gain, norm2_shift]
+    )
+    outputs, full, qkvc, logs, mid_half, act, dge, nhat, rstd, d_second, small = forward_call(
+        depth, tokens, segment, cotangent, query_w, key_w, value_w, attn_out_w, up_w, jnp.transpose(down_w),
+        short, up_bias[None],
+    )
+    d_tokens, qw, kw, vw, ow, uw, dw, short_sum, up_sum = backward_call(
+        depth, tokens, segment, full, qkvc, logs, mid_half, act, dge, nhat, rstd, d_second, small
+    )
+    qb, vb, ob, db, g1, s1, g2, s2 = short_sum[:, : query_w.shape[0]]
+    return (
+        outputs, d_tokens, qw, kw, vw, ow, uw, jnp.transpose(dw), qb, vb, ob, up_sum[0], db, g1, s1, g2, s2,
+    )
+
+
 def solution(mesh):
+    fits = mesh.shape["fsdp"] == 4 and mesh.shape["dp"] % 2 == 0 and 1024 // mesh.size == 32
+    body = kernel_device if fits else plain_device
     in_specs = (
         P(("dp", "fsdp"), None),
         P(("dp", "fsdp"), None),
@@ -410,5 +1257,5 @@
         P(("dp", "fsdp")),
     )
     return jax.shard_map(
-        per_device, mesh=mesh, in_specs=in_specs, out_specs=out_specs, check_vma=False
-    )
+        body, mesh=mesh, in_specs=in_specs, out_specs=out_specs, check_vma=False
+    )

time: 1220 us -> 272 us (0.22)
  waiting for transfers between devices: 836 us -> 0 us
  Pallas kernels: 0 us -> 259 us
  matrix products: 157 us -> 0 us
  blocking collectives: 124 us -> 0 us
  other arithmetic: 49.4 us -> 0 us
  local copies, waits for them, and re-layouts: 33.4 us -> 11.8 us
  between operations: 18.1 us -> 0.75 us
    reduce_scatter x6 -> x0, waiting for transfers between devices: 446 us -> none  [the longest x1 152 us: per_device(): lax.psum_scatter(members[5].astype(jnp.bfloat16), 'dp', scatter_dimension...]
    pallas_call x0 -> x2, Pallas kernels: none -> 259 us  [the longest x1 130 us: backward_call(): pl.pallas_call(functools.partial(backward_kernel, depth), out_shape=tuple...]
    all_gather x6 -> x0, waiting for transfers between devices: 227 us -> none  [the longest x1 74.9 us: per_device(): lax.all_gather(to_half(up_w), ('dp', 'fsdp'), axis=0, tiled=True)]
    unnamed x24 -> x0, waiting for transfers between devices: 163 us -> none
    dot_general x24 -> x0, matrix products: 157 us -> none  [the longest x6 50.2 us: matmul(): return jnp.dot(left, right, preferred_element_type=jnp.float32)]
    unnamed x3 -> x0, blocking collectives: 83.3 us -> none
    all_gather x1 -> x0, blocking collectives: 40.3 us -> none  [per_device(): lax.all_gather(to_half(up_bias), ('dp', 'fsdp'), axis=0, tiled=True)]
    convert_element_type x32 -> x0, other arithmetic: 30.2 us -> none  [the longest x15 23.2 us: to_half(): return array.astype(jnp.bfloat16)]
  transfers between devices with their start and end apart: 18 -> 0, of which waited for: 15 -> 0; matrix products, arithmetic and copies ran while one was open for 13% -> 0% of each run, Pallas kernels for 0% -> 0%
where the time goes in v2:
time: 272 us
  Pallas kernels  259 us (95%)
  local copies, waits for them, and re-layouts  11.8 us (4%)
    pallas_call x1, Pallas kernels, backward_call(): pl.pallas_call(functools.partial(backward_kernel, depth), out_shape=tuple...  130 us
    pallas_call x1, Pallas kernels, forward_call(): pl.pallas_call(functools.partial(forward_kernel, depth), out_shape=tuple(...  130 us
    unnamed x25, local copies, waits for them, and re-layouts  8.88 us

profile of v2, /device:TPU:0, one launch (start us, length us, event | category | flops | bytes accessed | tf_op | source)
XLA Modules:
  0.0 271.8 jit_solution(2494136094616979909)
XLA Ops:
  0.7 1.4 stack.35.short_in
  2.0 129.6 %forward.1 = (bf16[512,1024]{1,0:T(8,128)(2,1)}, bf16[12,4,2,2,2,32,1024]{6,5,4,3,2,1,0:T(8,128)(2,1)}, bf16[4,512,1024]{2,1,0:T(8,128)(2,1)}, f32[128,512]{1,0:...) custom-call(bf16[512,1024]{1,0:T(8,128)(2,1)} %tokens_hbm.1, ...), custom_call_target="tpu_custom_call" | custom-call | tf_op jit(solution)/shard_map/forward/pallas_call | solution.py:782
  131.6 0.0 copy-start
  131.6 129.7 %backward.1 = (f32[512,1024]{1,0:T(8,128)}, f32[32,1024]{1,0:T(8,128)}, f32[32,1024]{1,0:T(8,128)}, f32[32,1024]{1,0:T(8,128)}, f32[32,1024]{1,0:T(8,128)}, /*in...) custom-call(bf16[512,1024]{1,0:T(8,128)(2,1)} %tokens_hbm.1, s32[1,512]{1,0:T(1,128)} %segment.3, ...), custom_call_target="tpu_custom_call" | custom-call | tf_op jit(solution)/shard_map/backward/pallas_call | solution.py:1183
  261.3 0.0 copy-start.6
  261.3 0.0 copy-start.5
  261.4 0.0 copy-start.4
  261.4 0.0 copy-start.3
  261.4 0.0 copy-start.2
  261.4 1.5 slice_bitcast_fusion
  262.9 0.0 copy-done
  262.9 0.0 copy-start.1
  262.9 0.0 copy-start.7
  262.9 1.0 copy.44
  263.9 3.2 %copy.45 = f32[512,1024]{1,0:T(8,128)} copy(f32[512,1024]{1,0:T(8,128)} %get-tuple-element.83) | data formatting | bytes 4194304
  267.1 0.7 copy.46
  267.7 0.7 copy.47
  268.4 0.7 copy.48
  269.0 0.0 copy-done.3
  269.0 0.7 copy.49
  269.7 0.0 copy-done.2
  269.7 0.8 copy.50
  270.5 0.8 copy.51
  271.3 0.5 copy.52
  (5 shorter events, 0.0 us)
Async XLA Ops:
  131.6 131.3 %copy-start = (bf16[512,1024]{1,0:T(8,128)(2,1)S(1)}, bf16[512,1024]{1,0:T(8,128)(2,1)}, u32[]{:S(2)}) copy-start(bf16[512,1024]{1,0:T(8,128)(2,1)} %get-tuple-element.82) | copy-start | bytes 3145732
  261.3 5.7 %copy-start.6 = (f32[32,1024]{1,0:T(8,128)S(1)}, f32[32,1024]{1,0:T(8,128)}, u32[]{:S(2)}) copy-start(f32[32,1024]{1,0:T(8,128)} %get-tuple-element.84) | copy-start | bytes 393220
  261.3 6.4 %copy-start.5 = (f32[32,1024]{1,0:T(8,128)S(1)}, f32[32,1024]{1,0:T(8,128)}, u32[]{:S(2)}) copy-start(f32[32,1024]{1,0:T(8,128)} %get-tuple-element.85) | copy-start | bytes 393220
  261.4 7.0 %copy-start.4 = (f32[32,1024]{1,0:T(8,128)S(1)}, f32[32,1024]{1,0:T(8,128)}, u32[]{:S(2)}) copy-start(f32[32,1024]{1,0:T(8,128)} %get-tuple-element.86) | copy-start | bytes 393220
  261.4 7.7 %copy-start.3 = (f32[32,1024]{1,0:T(8,128)S(1)}, f32[32,1024]{1,0:T(8,128)}, u32[]{:S(2)}) copy-start(f32[32,1024]{1,0:T(8,128)} %get-tuple-element.87) | copy-start | bytes 393220
  261.4 8.3 %copy-start.2 = (f32[32,4096]{1,0:T(8,128)S(1)}, f32[32,4096]{1,0:T(8,128)}, u32[]{:S(2)}) copy-start(f32[32,4096]{1,0:T(8,128)} %get-tuple-element.88) | copy-start | bytes 1572868
  262.9 7.6 %copy-start.1 = (f32[32,4096]{1,0:T(8,128)S(1)}, f32[32,4096]{1,0:T(8,128)}, u32[]{:S(2)}) copy-start(f32[32,4096]{1,0:T(8,128)} %get-tuple-element.54) | copy-start | bytes 1572868
  262.9 8.4 %copy-start.7 = (f32[1,128]{1,0:T(1,128)S(1)}, f32[1,128]{1,0:T(1,128)}, u32[]{:S(2)}) copy-start(f32[1,128]{1,0:T(1,128)} %get-tuple-element.56) | copy-start | bytes 1540
